TPU v7x, 32 devices: a whole 2x2x4 slice. The times are simulated.
32 devices in a mesh: rows: 8 (over z, x), cols: 4 (over y, core).
Axes of the slice: x: 2, y: 2, z: 4, core: 2. Of those that a mesh axis runs over, the one named last changes fastest.
Arguments:
- tile_density: bfloat16 [2048, 64, 64], P(('rows', 'cols')), may hold values from -6 to 6
- tile_dest: int32 [2048, 1], P(('rows', 'cols')), may hold values from 0 to 7; in each aligned block of 64 rows (0 to 63, 64 to 127, ...) at most 16 rows name the same one
- tile_place: int32 [2048], P(('rows', 'cols')), may hold values from 0 to 31
- psf_spectrum: bfloat16 [2048, 2048], P('rows', 'cols'), may hold values from 0.049804688 to 1
Outputs:
- flare_spectrum: float32 [2048, 2, 2048], P('rows', None, 'cols')
Inputs may be any that keep to these rules, and one draw needn't show every extreme that they name: `tile_dest`: among the 64 tiles of one owner, at most 16 lie in the same row slab, and some owner has exactly 16 in one row slab.
All inputs are finite; a program needn't handle non-finite values.
Results may differ from a plain program's by a relative error of at most 0.0075.
Values may be sent and summed in bfloat16 or wider, within the bound.
A program may use at most 64 MiB of HBM per device.

v0:
```python
import math

import jax
import jax.numpy as jnp
from jax import lax
from jax.sharding import PartitionSpec as P


def make_table(length, factor):
    positions = jnp.arange(length, dtype=jnp.int32)
    angles = (
        2.0
        * math.pi
        / length
        * (positions[:, None] * positions[None, :] % length).astype(jnp.float32)
    )
    cosine = jnp.cos(angles) * factor
    sine_part = jnp.sin(angles) * factor
    upper_rows = jnp.stack([cosine, -sine_part], 1)
    bottom = jnp.stack([sine_part, cosine], 1)
    return jnp.stack([upper_rows, bottom], 0).astype(jnp.bfloat16)


def twiddle(real_part, imag_part, position, frequency, period):
    angles = 2.0 * math.pi / period * (position * frequency % period).astype(jnp.float32)
    cosine = jnp.cos(angles)
    sine_part = jnp.sin(angles)
    return (real_part * cosine + imag_part * sine_part, imag_part * cosine - real_part * sine_part)


def on_device(tile_density, tile_dest, tile_place, psf_spectrum):
    tile_count, tile_side, _ = tile_density.shape
    rows_dev, cols_dev = psf_spectrum.shape
    rows_n = lax.axis_size("rows")
    cols_n = lax.axis_size("cols")
    capacity = max(2, 2 * tile_count // rows_n)
    slot_total = rows_n * capacity
    target = tile_dest[:, 0]
    matches = (target[:, None] == jnp.arange(rows_n, dtype=jnp.int32)[None, :]).astype(jnp.int32)
    order_within = jnp.sum((jnp.cumsum(matches, 0) - matches) * matches, 1)
    slot_index = target * capacity + order_within
    chosen = slot_index[:, None] == jnp.arange(slot_total, dtype=jnp.int32)[None, :]
    tiles_flat = tile_density.reshape(tile_count, tile_side * tile_side)
    outgoing = jnp.einsum(
        "ts,tc->sc", chosen.astype(jnp.bfloat16), tiles_flat, preferred_element_type=jnp.float32
    ).astype(jnp.bfloat16)
    labels = jnp.sum(jnp.where(chosen, (tile_place + 1)[:, None], 0), axis=0)
    arrived, arrived_marks = (
        lax.all_to_all(outgoing, "rows", split_axis=0, concat_axis=0, tiled=True),
        lax.all_to_all(labels, "rows", split_axis=0, concat_axis=0, tiled=True),
    )
    per_row = cols_dev // tile_side
    positions_count = rows_dev // tile_side * per_row
    placement_hot = (
        arrived_marks[:, None] - 1 == jnp.arange(positions_count, dtype=jnp.int32)[None, :]
    ).astype(jnp.bfloat16)
    cell_tiles = jnp.einsum(
        "sp,sc->pc", placement_hot, arrived, preferred_element_type=jnp.float32
    ).astype(jnp.bfloat16)
    density_grid = cell_tiles.reshape(
        rows_dev // tile_side, per_row, tile_side, tile_side
    ).transpose(0, 2, 1, 3)
    density_grid = density_grid.reshape(rows_dev, cols_dev)
    me_col = lax.axis_index("cols")
    highest = lax.Precision.HIGHEST
    slab_cols = cols_dev * cols_n
    part_cols = cols_dev // cols_n
    pieces = lax.all_to_all(density_grid[None], "cols", split_axis=2, concat_axis=0, tiled=True)
    frequency = jnp.arange(cols_n, dtype=jnp.int32)
    angles = (
        2.0
        * math.pi
        / cols_n
        * (frequency[:, None] * frequency[None, :] % cols_n).astype(jnp.float32)
    )
    values = pieces.astype(jnp.float32)
    sum_real = jnp.einsum("ejt,ek->kjt", values, jnp.cos(angles), precision=highest)
    sum_imag = -jnp.einsum("ejt,ek->kjt", values, jnp.sin(angles), precision=highest)
    columns = (me_col * part_cols + jnp.arange(part_cols, dtype=jnp.int32))[None, None, :]
    real_part, imag_part = twiddle(sum_real, sum_imag, columns, frequency[:, None, None], slab_cols)
    packed = jnp.stack([real_part, imag_part], 2).astype(jnp.bfloat16)
    returned = lax.all_to_all(packed, "cols", split_axis=0, concat_axis=3, tiled=True)
    section_one = returned.reshape(rows_dev, 2 * cols_dev)
    row_table = make_table(cols_dev, 1.0 / math.sqrt(slab_cols)).reshape(2 * cols_dev, 2 * cols_dev)
    rows_spectrum = jnp.dot(section_one, row_table, preferred_element_type=jnp.float32).astype(
        jnp.bfloat16
    )
    rows_spectrum = rows_spectrum.reshape(rows_dev, 2, cols_dev)
    me_row = lax.axis_index("rows")
    group_rows = rows_dev // rows_n
    grid_rows = rows_dev * rows_n
    col_table = make_table(rows_n, 1.0).transpose(3, 2, 1, 0)
    column_block = lax.all_to_all(rows_spectrum, "rows", split_axis=0, concat_axis=0, tiled=True)
    item_width = column_block.shape[2]
    values = column_block.reshape(rows_n, group_rows, 2, item_width)
    combined = jnp.einsum("kqap,atpc->ktqc", col_table, values, preferred_element_type=jnp.float32)
    row_index = (me_row * group_rows + jnp.arange(group_rows, dtype=jnp.int32))[None, :, None]
    row_freq = jnp.arange(rows_n, dtype=jnp.int32)[:, None, None]
    real_two, imag_two = twiddle(
        combined[:, :, 0], combined[:, :, 1], row_index, row_freq, grid_rows
    )
    section_two = lax.all_to_all(
        jnp.stack([real_two, imag_two], 2).astype(jnp.bfloat16).reshape(rows_dev, 2, item_width),
        "rows",
        split_axis=0,
        concat_axis=0,
        tiled=True,
    )
    final_table = (
        make_table(rows_dev, 1.0 / math.sqrt(grid_rows))
        .transpose(3, 2, 1, 0)
        .reshape(2 * rows_dev, 2 * rows_dev)
    )
    result_spec = jnp.dot(
        final_table, section_two.reshape(2 * rows_dev, cols_dev), preferred_element_type=jnp.float32
    )
    result_spec = result_spec.reshape(rows_dev, 2, cols_dev)
    return result_spec * psf_spectrum.astype(jnp.float32)[:, None, :]


def solution(mesh):
    in_specs = (
        P(("rows", "cols"), None, None),
        P(("rows", "cols"), None),
        P(("rows", "cols")),
        P("rows", "cols"),
    )
    out_specs = P("rows", None, "cols")
    return jax.shard_map(
        on_device, mesh=mesh, in_specs=in_specs, out_specs=out_specs, check_vma=False
    )
```

profile of v0, /device:TPU:0, one launch (start us, length us, event | category | flops | bytes accessed | tf_op | source)
XLA Modules:
  0.0 119.4 jit_solution(17605546061817330501)
XLA Ops:
  0.0 0.7 fusion.26
  0.8 0.8 select_reduce_fusion.1
  1.7 0.7 fusion.60
  2.3 0.7 broadcast_add_fusion
  3.1 0.7 all_to_all.44
  3.8 7.3 %all-to-all-start = ((s32[8,16,1]{1,2,0:T(1,128)}), s32[8,16,1]{1,2,0:T(1,128)S(1)}, u32[]{:S(2)}, u32[]{:S(2)}) async-start(s32[8,16,1]{1,2,0:T(1,128)} %bitcast.8), calls=%async_computation | async-start | bytes 8192 | tf_op jit(solution)/shard_map/all_to_all | solution.py:50
  11.0 2.1 %reshape.423 = bf16[64,4096]{1,0:T(8,128)(2,1)S(1)} reshape(bf16[64,64,64]{2,1,0:T(8,128)(2,1)} %param.4) | data formatting | bytes 1048576 | tf_op jit(solution)/shard_map/reshape | solution.py:43
  13.1 1.5 %convolution_convert_fusion = bf16[128,4096]{1,0:T(8,128)(2,1)} fusion(bf16[64,4096]{1,0:T(8,128)(2,1)S(1)} %reshape.423, s32[64]{0:T(128)S(1)} %fusion.60), kind=kOutput, calls=%fused_computation | convolution fusion | flops 67641344 | bytes 1573120 | tf_op jit(solution)/shard_map/ts,tc->sc/dot_general | solution.py:44
  14.6 2.9 %all-to-all-done = s32[8,16,1]{1,2,0:T(1,128)S(1)} async-done(((s32[8,16,1]{1,2,0:T(1,128)}), s32[8,16,1]{1,2,0:T(1,128)S(1)}, u32[]{:S(2)}, u32[]{:S(2)}) %all-to-all-start) | async-done | bytes 544 | tf_op jit(solution)/shard_map/all_to_all | solution.py:50
  17.5 3.6 %all-to-all-start.1 = ((bf16[8,16,4096]{2,1,0:T(8,128)(2,1)}), bf16[8,16,4096]{2,1,0:T(8,128)(2,1)S(1)}, u32[]{:S(2)}, u32[]{:S(2)}) async-start(bf16[8,16,4096]{2,1,0:T(8,128)(2,1)} %bitcast.9), calls=%async_computation.1 | async-start | bytes 2097152 | tf_op jit(solution)/shard_map/all_to_all | solution.py:49
  21.1 4.4 %negate_convert_fusion = (bf16[512,1,512]{2,0,1:T(8,128)(2,1)S(1)}, bf16[512,1,512]{2,0,1:T(8,128)(2,1)S(1)}) fusion(), kind=kLoop, calls=%fused_computation.16 | loop fusion | flops 4980736 | bytes 1048576 | tf_op jit(solution)/shard_map/convert.19
  25.6 20.5 %all-to-all-done.1 = bf16[8,16,4096]{2,1,0:T(8,128)(2,1)S(1)} async-done(((bf16[8,16,4096]{2,1,0:T(8,128)(2,1)}), bf16[8,16,4096]{2,1,0:T(8,128)(2,1)S(1)}, u32[]{:S(2)}, u32[]{:S(2)}) %all-to-all-start.1) | async-done | bytes 1048608 | tf_op jit(solution)/shard_map/all_to_all | solution.py:49
  48.6 2.2 %reduce.4 = bf16[512,256]{1,0:T(8,128)(2,1)S(1)} reduce(bf16[512,1,256]{2,1,0:T(2,128)(2,1)S(1)} %bitcast.96, bf16[]{:T(256)} %broadcast.613), dimensions={1}, to_apply=%bitcast.80.reduce_sub_computation | reduce | bytes 524290
  50.8 0.8 reshape.443
  51.6 3.4 %all-to-all-start.2 = ((bf16[4,2,16384]{2,1,0:T(2,128)(2,1)}), bf16[4,2,16384]{2,1,0:T(2,128)(2,1)S(1)}, u32[]{:S(2)}, u32[]{:S(2)}) async-start(bf16[4,2,16384]{2,1,0:T(2,128)(2,1)} %reshape.443), calls=%async_computation.2 | async-start | bytes 524288 | tf_op jit(solution)/shard_map/all_to_all | solution.py:68
  55.1 5.9 %all-to-all-done.2 = bf16[4,2,16384]{2,1,0:T(2,128)(2,1)S(1)} async-done(((bf16[4,2,16384]{2,1,0:T(2,128)(2,1)}), bf16[4,2,16384]{2,1,0:T(2,128)(2,1)S(1)}, u32[]{:S(2)}, u32[]{:S(2)}) %all-to-all-start.2) | async-done | bytes 262176 | tf_op jit(solution)/shard_map/all_to_all | solution.py:68
  62.1 0.8 fusion.16
  63.4 0.9 copy.72
  64.2 3.7 %all-to-all-start.3 = ((bf16[4,256,2,128]{3,1,2,0:T(8,128)(2,1)}), bf16[4,256,2,128]{3,1,2,0:T(8,128)(2,1)S(1)}, u32[]{:S(2)}, u32[]{:S(2)}) async-start(bf16[4,256,2,128]{3,1,2,0:T(8,128)(2,1)} %copy.72), calls=%async_computation.3 | async-start | bytes 1048576 | tf_op jit(solution)/shard_map/all_to_all | solution.py:82
  67.9 4.0 %fusion.7 = bf16[512,1,512]{2,0,1:T(8,128)(2,1)S(1)} fusion(), kind=kLoop, calls=%fused_computation.22 | loop fusion | flops 4194304 | bytes 524288 | tf_op jit(solution)/shard_map/convert.15
  72.3 2.2 %copy.74 = bf16[2,512,2,512]{3,2,1,0:T(2,128)(2,1)S(1)} copy(bf16[2,512,2,512]{3,1,2,0:T(8,128)(2,1)S(1)} %pad_maximum_fusion) | data formatting | bytes 4194304 | tf_op jit(solution)/shard_map/stack | solution.py:21
  75.0 1.5 %all-to-all-done.3 = bf16[4,256,2,128]{3,1,2,0:T(8,128)(2,1)S(1)} async-done(((bf16[4,256,2,128]{3,1,2,0:T(8,128)(2,1)}), bf16[4,256,2,128]{3,1,2,0:T(8,128)(2,1)S(1)}, u32[]{:S(2)}, u32[]{:S(2)}) %all-to-all-start.3) | async-done | bytes 524320 | tf_op jit(solution)/shard_map/all_to_all | solution.py:82
  76.7 0.7 convolution_convert_fusion.2
  77.5 1.2 reshape.426
  78.7 3.5 %all-to-all-start.4 = ((bf16[256,2,512]{2,1,0:T(2,128)(2,1)}), bf16[256,2,512]{2,1,0:T(2,128)(2,1)S(1)}, u32[]{:S(2)}, u32[]{:S(2)}) async-start(bf16[256,2,512]{2,1,0:T(2,128)(2,1)} %reshape.426), calls=%async_computation.4 | async-start | bytes 1048576 | tf_op jit(solution)/shard_map/all_to_all | solution.py:93
  82.6 14.0 %all-to-all-done.4 = bf16[256,2,512]{2,1,0:T(2,128)(2,1)S(1)} async-done(((bf16[256,2,512]{2,1,0:T(2,128)(2,1)}), bf16[256,2,512]{2,1,0:T(2,128)(2,1)S(1)}, u32[]{:S(2)}, u32[]{:S(2)}) %all-to-all-start.4) | async-done | bytes 524320 | tf_op jit(solution)/shard_map/all_to_all | solution.py:93
  97.5 1.3 %copy.81 = bf16[256,2,512]{2,1,0:T(2,128)(2,1)} copy(bf16[256,2,512]{2,0,1:T(8,128)(2,1)S(1)} %pad_maximum_fusion.2) | data formatting | bytes 1048576 | tf_op jit(solution)/shard_map/stack | solution.py:103
  98.9 3.6 %all-to-all-start.5 = ((bf16[256,2,512]{2,1,0:T(2,128)(2,1)}), bf16[256,2,512]{2,1,0:T(2,128)(2,1)S(1)}, u32[]{:S(2)}, u32[]{:S(2)}) async-start(bf16[256,2,512]{2,1,0:T(2,128)(2,1)} %copy.81), calls=%async_computation.5 | async-start | bytes 1048576 | tf_op jit(solution)/shard_map/all_to_all | solution.py:102
  102.5 1.0 fusion.24
  103.5 1.1 negate_convert_fusion.1
  104.7 12.4 %all-to-all-done.5 = bf16[256,2,512]{2,1,0:T(2,128)(2,1)S(1)} async-done(((bf16[256,2,512]{2,1,0:T(2,128)(2,1)}), bf16[256,2,512]{2,1,0:T(2,128)(2,1)S(1)}, u32[]{:S(2)}, u32[]{:S(2)}) %all-to-all-start.5) | async-done | bytes 524320 | tf_op jit(solution)/shard_map/all_to_all | solution.py:102
  117.6 1.8 %copy.83 = f32[256,2,512]{2,1,0:T(2,128)} copy(f32[256,2,512]{2,0,1:T(8,128)S(1)} %fusion) | data formatting | bytes 2097152 | tf_op jit(solution)/shard_map/mul | solution.py:118
  (38 shorter events, 7.3 us)
Async XLA Ops:
  3.8 13.7 %all-to-all-start = ((s32[8,16,1]{1,2,0:T(1,128)}), s32[8,16,1]{1,2,0:T(1,128)S(1)}, u32[]{:S(2)}, u32[]{:S(2)}) async-start(s32[8,16,1]{1,2,0:T(1,128)} %bitcast.8), calls=%async_computation | async-start | bytes 8192 | tf_op jit(solution)/shard_map/all_to_all | solution.py:50
  17.5 28.6 %all-to-all-start.1 = ((bf16[8,16,4096]{2,1,0:T(8,128)(2,1)}), bf16[8,16,4096]{2,1,0:T(8,128)(2,1)S(1)}, u32[]{:S(2)}, u32[]{:S(2)}) async-start(bf16[8,16,4096]{2,1,0:T(8,128)(2,1)} %bitcast.9), calls=%async_computation.1 | async-start | bytes 2097152 | tf_op jit(solution)/shard_map/all_to_all | solution.py:49
  51.6 9.4 %all-to-all-start.2 = ((bf16[4,2,16384]{2,1,0:T(2,128)(2,1)}), bf16[4,2,16384]{2,1,0:T(2,128)(2,1)S(1)}, u32[]{:S(2)}, u32[]{:S(2)}) async-start(bf16[4,2,16384]{2,1,0:T(2,128)(2,1)} %reshape.443), calls=%async_computation.2 | async-start | bytes 524288 | tf_op jit(solution)/shard_map/all_to_all | solution.py:68
  64.2 12.3 %all-to-all-start.3 = ((bf16[4,256,2,128]{3,1,2,0:T(8,128)(2,1)}), bf16[4,256,2,128]{3,1,2,0:T(8,128)(2,1)S(1)}, u32[]{:S(2)}, u32[]{:S(2)}) async-start(bf16[4,256,2,128]{3,1,2,0:T(8,128)(2,1)} %copy.72), calls=%async_computation.3 | async-start | bytes 1048576 | tf_op jit(solution)/shard_map/all_to_all | solution.py:82
  78.7 18.0 %all-to-all-start.4 = ((bf16[256,2,512]{2,1,0:T(2,128)(2,1)}), bf16[256,2,512]{2,1,0:T(2,128)(2,1)S(1)}, u32[]{:S(2)}, u32[]{:S(2)}) async-start(bf16[256,2,512]{2,1,0:T(2,128)(2,1)} %reshape.426), calls=%async_computation.4 | async-start | bytes 1048576 | tf_op jit(solution)/shard_map/all_to_all | solution.py:93
  97.3 5.2 %copy-start = (bf16[256,512]{1,0:T(8,128)(2,1)S(1)}, bf16[256,512]{1,0:T(8,128)(2,1)}, u32[]{:S(2)}) copy-start(bf16[256,512]{1,0:T(8,128)(2,1)} %param.7) | copy-start | bytes 786436
  98.9 18.3 %all-to-all-start.5 = ((bf16[256,2,512]{2,1,0:T(2,128)(2,1)}), bf16[256,2,512]{2,1,0:T(2,128)(2,1)S(1)}, u32[]{:S(2)}, u32[]{:S(2)}) async-start(bf16[256,2,512]{2,1,0:T(2,128)(2,1)} %copy.81), calls=%async_computation.5 | async-start | bytes 1048576 | tf_op jit(solution)/shard_map/all_to_all | solution.py:102
where the time goes:
time: 120 us; the launch traced here: 119 us
  waiting for transfers between devices  57.2 us (48%)
  starting transfers between devices  25 us (21%)
  other arithmetic  17.2 us (14%)
  local copies, waits for them, and re-layouts  14.7 us (12%)
  matrix products  4.97 us (4%)
    all_to_all x1, waiting for transfers between devices, on_device(): lax.all_to_all(outgoing, 'rows', split_axis=0, concat_axis=0, tiled=True)  20.5 us
    all_to_all x1, waiting for transfers between devices, on_device(): lax.all_to_all(rows_spectrum, 'rows', split_axis=0, concat_axis=0, tiled=...  14 us
    all_to_all x1, waiting for transfers between devices, on_device(): lax.all_to_all(jnp.stack([real_two, imag_two], 2).astype(jnp.bfloat16).re...  12.4 us
    another operation x7, other arithmetic  10.8 us
    all_to_all x1, starting transfers between devices, on_device(): lax.all_to_all(labels, 'rows', split_axis=0, concat_axis=0, tiled=True)  7.25 us
    all_to_all x1, waiting for transfers between devices, on_device(): lax.all_to_all(density_grid[None], 'cols', split_axis=2, concat_axis=0, t...  5.95 us
    all_to_all x1, starting transfers between devices, on_device(): lax.all_to_all(packed, 'cols', split_axis=0, concat_axis=3, tiled=True)  3.65 us
    all_to_all x1, starting transfers between devices, on_device(): lax.all_to_all(jnp.stack([real_two, imag_two], 2).astype(jnp.bfloat16).re...  3.62 us
  transfers between devices with their start and end apart: 6, of which 6 were waited for; matrix products, arithmetic and copies ran while one was open for 15% of the time, Pallas kernels for 0%

commit v1 on v0

--- a/solution.py
+++ b/solution.py
@@ -1,8 +1,12 @@
+import functools
 import math
 
 import jax
 import jax.numpy as jnp
+import numpy as np
 from jax import lax
+from jax.experimental import pallas as pl
+from jax.experimental.pallas import tpu as pltpu
 from jax.sharding import PartitionSpec as P
 
 
@@ -118,6 +122,320 @@
     return result_spec * psf_spectrum.astype(jnp.float32)[:, None, :]
 
 
+CHUNKS = 2
+MESH = pl.DeviceIdType.MESH
+
+
+def fits(rows_n, cols_n, tile_count, tile_side, rows_dev, cols_dev):
+    return (
+        cols_n == 4
+        and rows_n > 1
+        and tile_side * 2 == 128
+        and tile_side % (rows_n * 2 * CHUNKS) == 0
+        and tile_count % 16 == 0
+        and tile_count <= 128
+        and cols_dev % 128 == 0
+        and rows_dev % tile_side == 0
+        and (tile_side // rows_n // CHUNKS) * (rows_dev // tile_side) % 16 == 0
+        and rows_n * rows_dev * cols_dev * 2 <= 1 << 22
+    )
+
+
+def constants(rows_n, cols_n, tile_side, rows_dev, cols_dev):
+    slab_cols, grid_rows = cols_dev * cols_n, rows_dev * rows_n
+    bands = rows_dev // tile_side
+    band_rows = tile_side // rows_n
+    step_rows = band_rows // CHUNKS
+
+    def parts(phase, factor):
+        angles = 2.0 * np.pi * phase
+        return np.cos(angles) * factor, -np.sin(angles) * factor
+
+    f = np.arange(cols_dev)
+    re, im = parts((f[:, None] * f[None, :] % cols_dev) / cols_dev, 1.0 / math.sqrt(slab_cols))
+    row_table = np.block([[re, im], [-im, re]])
+    k = np.arange(cols_n)
+    re, im = parts((f[None, :] * k[:, None] % slab_cols) / slab_cols, 1.0)
+    twiddles = np.stack([re, -im], 1).astype(np.float32)
+    b = (
+        tile_side * np.arange(bands)[None, None, None, :]
+        + band_rows * np.arange(rows_n)[:, None, None, None]
+        + step_rows * np.arange(CHUNKS)[None, :, None, None]
+        + np.arange(step_rows)[None, None, :, None]
+    )
+    u = np.arange(rows_n)
+    row = b[:, :, None, None] + rows_dev * u[None, None, None, :, None, None]
+    re, im = parts((row * u[None, None, :, None, None, None] % grid_rows) / grid_rows, 1.0)
+    width = step_rows * bands
+    mix = np.zeros((rows_n, CHUNKS, rows_n, 2, step_rows, bands, 2, step_rows, rows_n, bands), np.float32)
+    for i in range(step_rows):
+        for t in range(bands):
+            mix[:, :, :, 0, i, t, 0, i, :, t] = re[:, :, :, :, i, t]
+            mix[:, :, :, 0, i, t, 1, i, :, t] = -im[:, :, :, :, i, t]
+            mix[:, :, :, 1, i, t, 0, i, :, t] = im[:, :, :, :, i, t]
+            mix[:, :, :, 1, i, t, 1, i, :, t] = re[:, :, :, :, i, t]
+    mix = mix.reshape(rows_n, CHUNKS, rows_n * 2 * width, 2 * rows_n * width)
+    w = np.arange(rows_dev)
+    order = b.transpose(1, 0, 2, 3).reshape(CHUNKS, rows_n, 1, width)
+    re, im = parts(
+        (w[:, None, None, None, None] * order % rows_dev) / rows_dev, 1.0 / math.sqrt(grid_rows)
+    )
+    final = np.stack(
+        [np.concatenate([re, -im], 3), np.concatenate([im, re], 3)], 0
+    ).reshape(2 * rows_dev, 2 * rows_dev)
+    return (
+        jnp.asarray(row_table.astype(jnp.bfloat16)),
+        jnp.asarray(twiddles),
+        jnp.asarray(mix.astype(jnp.bfloat16)),
+        jnp.asarray(final.astype(jnp.bfloat16)),
+    )
+
+
+def exchange_kernel(
+    rows_n, cols_n, tile_side, bands, per_row,
+    x_ref, dest_ref, place_ref, twiddle_ref, table_hbm, mix_hbm,
+    out_ref,
+    labels, arrived, dense, outgoing, table, mix,
+    label_send, label_recv, a_send, a_recv, g_send, g_recv, e_send, e_recv, local_sem,
+):
+    me_row, me_col = lax.axis_index("rows"), lax.axis_index("cols")
+    tiles = x_ref.shape[0]
+    chunk = arrived.shape[3]
+    band = chunk * CHUNKS
+    cols_dev = per_row * tile_side
+    row_peers = [lax.rem(me_row + d, rows_n) for d in range(rows_n)]
+    row_sources = [lax.rem(me_row + rows_n - d, rows_n) for d in range(rows_n)]
+    col_peers = [lax.rem(me_col + d, cols_n) for d in range(cols_n)]
+
+    barrier = pltpu.get_barrier_semaphore()
+    for d in range(1, rows_n):
+        pl.semaphore_signal(barrier, inc=1, device_id=(row_peers[d], me_col), device_id_type=MESH)
+    for d in range(1, cols_n):
+        pl.semaphore_signal(barrier, inc=1, device_id=(me_row, col_peers[d]), device_id_type=MESH)
+
+    place = place_ref[...]
+    code = (place % per_row) * (rows_n * bands) + dest_ref[...] * bands + place // per_row
+    labels[0] = jnp.broadcast_to(
+        jnp.concatenate([code, jnp.zeros((1, 128 - tiles), jnp.int32)], 1)
+        if tiles < 128
+        else code,
+        labels.shape[1:],
+    )
+    pl.semaphore_wait(barrier, rows_n + cols_n - 2)
+
+    def band_copy(h, d):
+        start = pl.multiple_of(row_peers[d] * band + h * chunk, 128)
+        return pltpu.make_async_remote_copy(
+            src_ref=x_ref.at[:, pl.ds(start, chunk)],
+            dst_ref=arrived.at[h, d],
+            send_sem=a_send.at[h, d],
+            recv_sem=a_recv.at[h, d],
+            device_id=(row_peers[d], me_col),
+            device_id_type=MESH,
+        )
+
+    label_copies = [
+        pltpu.make_async_remote_copy(
+            src_ref=labels.at[0],
+            dst_ref=labels.at[d],
+            send_sem=label_send.at[d],
+            recv_sem=label_recv.at[d],
+            device_id=(row_peers[d], me_col),
+            device_id_type=MESH,
+        )
+        for d in range(1, rows_n)
+    ]
+    band_copies = [[band_copy(h, d) for d in range(1, rows_n)] for h in range(CHUNKS)]
+    for copy in label_copies + [copy for group in band_copies for copy in group]:
+        copy.start()
+    own_copies = []
+    for h in range(CHUNKS):
+        start = pl.multiple_of(me_row * band + h * chunk, 128)
+        own_copies.append(
+            pltpu.make_async_copy(
+                x_ref.at[:, pl.ds(start, chunk)], arrived.at[h, 0], local_sem.at[h]
+            )
+        )
+    table_copy = pltpu.make_async_copy(table_hbm, table, local_sem.at[CHUNKS])
+    mix_copy = pltpu.make_async_copy(mix_hbm.at[me_row], mix, local_sem.at[CHUNKS + 1])
+    for copy in own_copies + [table_copy, mix_copy]:
+        copy.start()
+
+    for copy in label_copies:
+        copy.wait_recv()
+    codes = jnp.concatenate([labels[d, 0:1, 0:tiles] for d in range(rows_n)], 1)
+    cells = per_row * rows_n * bands
+    hot = jnp.where(
+        lax.broadcasted_iota(jnp.int32, (cells, rows_n * tiles), 0) == codes, 1.0, 0.0
+    ).astype(jnp.bfloat16)
+    low_lanes = lax.broadcasted_iota(jnp.int32, (rows_n * bands, 128), 1) < tile_side
+
+    gathers = []
+    for h in range(CHUNKS):
+        own_copies[h].wait()
+        for copy in band_copies[h]:
+            copy.wait_recv()
+        summed = jnp.dot(
+            hot,
+            arrived[h].reshape(rows_n * tiles, chunk),
+            preferred_element_type=jnp.float32,
+        )
+        height = rows_n * bands
+        for pair in range(chunk // 128):
+            lanes = slice(128 * pair, 128 * pair + 128)
+            for q in range(per_row // 2):
+                left = summed[2 * q * height : (2 * q + 1) * height, lanes]
+                right = summed[(2 * q + 1) * height : (2 * q + 2) * height, lanes]
+                upper = jnp.where(low_lanes, left, pltpu.roll(right, tile_side, 1))
+                lower = jnp.where(low_lanes, pltpu.roll(left, tile_side, 1), right)
+                out_lanes = slice(128 * q, 128 * q + 128)
+                first = 2 * pair * height
+                dense[h, 0, first : first + height, out_lanes] = upper.astype(jnp.bfloat16)
+                dense[h, 0, first + height : first + 2 * height, out_lanes] = lower.astype(
+                    jnp.bfloat16
+                )
+        group = [
+            pltpu.make_async_remote_copy(
+                src_ref=dense.at[h, 0],
+                dst_ref=dense.at[h, d],
+                send_sem=g_send.at[h, d],
+                recv_sem=g_recv.at[h, d],
+                device_id=(me_row, col_peers[d]),
+                device_id_type=MESH,
+            )
+            for d in range(1, cols_n)
+        ]
+        for copy in group:
+            copy.start()
+        gathers.append(group)
+
+    cosine = twiddle_ref[me_col, 0:1, :]
+    sine = twiddle_ref[me_col, 1:2, :]
+    table_copy.wait()
+    mix_copy.wait()
+    sends = []
+    for h in range(CHUNKS):
+        for copy in gathers[h]:
+            copy.wait_recv()
+        sum_real = sum_imag = None
+        for d in range(cols_n):
+            turn = lax.rem(lax.rem(me_col + cols_n - d, cols_n) * me_col, cols_n)
+            cos_turn = jnp.where(turn == 0, 1.0, jnp.where(turn == 2, -1.0, 0.0))
+            sin_turn = jnp.where(turn == 1, 1.0, jnp.where(turn == 3, -1.0, 0.0))
+            value = dense[h, d].astype(jnp.float32)
+            real, imag = value * cos_turn, value * (-sin_turn)
+            sum_real = real if d == 0 else sum_real + real
+            sum_imag = imag if d == 0 else sum_imag + imag
+        section_one = jnp.concatenate(
+            [sum_real * cosine + sum_imag * sine, sum_imag * cosine - sum_real * sine], 1
+        ).astype(jnp.bfloat16)
+        spectrum = jnp.dot(section_one, table[...], preferred_element_type=jnp.float32)
+        spectrum = spectrum.astype(jnp.bfloat16)
+        stacked = jnp.concatenate([spectrum[:, :cols_dev], spectrum[:, cols_dev:]], 0)
+        section_two = jnp.dot(mix[h], stacked, preferred_element_type=jnp.float32)
+        outgoing[h] = section_two.astype(jnp.bfloat16).reshape(outgoing.shape[1:])
+        group = [
+            pltpu.make_async_remote_copy(
+                src_ref=outgoing.at[h, row_peers[d]],
+                dst_ref=out_ref.at[h, me_row],
+                send_sem=e_send.at[h, d],
+                recv_sem=e_recv.at[h, d],
+                device_id=(row_peers[d], me_col),
+                device_id_type=MESH,
+            )
+            for d in range(1, rows_n)
+        ]
+        for copy in group:
+            copy.start()
+        own = pltpu.make_async_copy(
+            outgoing.at[h, me_row], out_ref.at[h, me_row], local_sem.at[CHUNKS + 2 + h]
+        )
+        own.start()
+        sends.append((group, own))
+
+    for copy in label_copies:
+        copy.wait_send()
+    for h in range(CHUNKS):
+        for copy in band_copies[h] + gathers[h]:
+            copy.wait_send()
+    for h in range(CHUNKS):
+        group, own = sends[h]
+        own.wait()
+        for d in range(1, rows_n):
+            pltpu.make_async_remote_copy(
+                src_ref=outgoing.at[h, row_peers[d]],
+                dst_ref=out_ref.at[h, row_sources[d]],
+                send_sem=e_send.at[h, d],
+                recv_sem=e_recv.at[h, d],
+                device_id=(row_peers[d], me_col),
+                device_id_type=MESH,
+            ).wait()
+
+
+def final_kernel(final_ref, section_ref, psf_ref, out_ref):
+    rows_dev = psf_ref.shape[0]
+    result = jnp.dot(final_ref[...], section_ref[...], preferred_element_type=jnp.float32)
+    psf = psf_ref[...].astype(jnp.float32)
+    out_ref[:, 0, :] = result[:rows_dev] * psf
+    out_ref[:, 1, :] = result[rows_dev:] * psf
+
+
+def on_device_kernels(tile_density, tile_dest, tile_place, psf_spectrum):
+    tile_count, tile_side, _ = tile_density.shape
+    rows_dev, cols_dev = psf_spectrum.shape
+    rows_n = lax.axis_size("rows")
+    cols_n = lax.axis_size("cols")
+    bands, per_row = rows_dev // tile_side, cols_dev // tile_side
+    step_rows = tile_side // rows_n // CHUNKS
+    chunk = step_rows * tile_side
+    row_table, twiddles, mix, final = constants(rows_n, cols_n, tile_side, rows_dev, cols_dev)
+    bf16 = jnp.bfloat16
+    vmem = pl.BlockSpec(memory_space=pltpu.VMEM)
+    anywhere = pl.BlockSpec(memory_space=pl.ANY)
+    width = 2 * step_rows * bands
+    dma = pltpu.SemaphoreType.DMA
+    section = pl.pallas_call(
+        functools.partial(exchange_kernel, rows_n, cols_n, tile_side, bands, per_row),
+        out_shape=jax.ShapeDtypeStruct((CHUNKS, rows_n, width, cols_dev), bf16),
+        in_specs=[vmem, vmem, vmem, vmem, anywhere, anywhere],
+        out_specs=vmem,
+        scratch_shapes=[
+            pltpu.VMEM((rows_n, 8, 128), jnp.int32),
+            pltpu.VMEM((CHUNKS, rows_n, tile_count, chunk), bf16),
+            pltpu.VMEM((CHUNKS, cols_n, step_rows * rows_n * bands, cols_dev), bf16),
+            pltpu.VMEM((CHUNKS, rows_n, width, cols_dev), bf16),
+            pltpu.VMEM(row_table.shape, bf16),
+            pltpu.VMEM(mix.shape[1:], bf16),
+            dma((rows_n,)),
+            dma((rows_n,)),
+            dma((CHUNKS, rows_n)),
+            dma((CHUNKS, rows_n)),
+            dma((CHUNKS, cols_n)),
+            dma((CHUNKS, cols_n)),
+            dma((CHUNKS, rows_n)),
+            dma((CHUNKS, rows_n)),
+            dma((2 * CHUNKS + 2,)),
+        ],
+        compiler_params=pltpu.CompilerParams(
+            collective_id=0, has_side_effects=True, vmem_limit_bytes=48 << 20
+        ),
+    )(
+        tile_density.reshape(tile_count, tile_side * tile_side),
+        tile_dest.reshape(1, tile_count),
+        tile_place.reshape(1, tile_count),
+        twiddles,
+        row_table,
+        mix,
+    )
+    return pl.pallas_call(
+        final_kernel,
+        out_shape=jax.ShapeDtypeStruct((rows_dev, 2, cols_dev), jnp.float32),
+        in_specs=[vmem, vmem, vmem],
+        out_specs=vmem,
+        compiler_params=pltpu.CompilerParams(vmem_limit_bytes=32 << 20),
+    )(final, section.reshape(2 * rows_dev, cols_dev), psf_spectrum)
+
+
 def solution(mesh):
     in_specs = (
         P(("rows", "cols"), None, None),
@@ -126,6 +444,17 @@
         P("rows", "cols"),
     )
     out_specs = P("rows", None, "cols")
+
+    def local(tile_density, tile_dest, tile_place, psf_spectrum):
+        fast = fits(
+            lax.axis_size("rows"),
+            lax.axis_size("cols"),
+            *tile_density.shape[:2],
+            *psf_spectrum.shape,
+        )
+        run = on_device_kernels if fast else on_device
+        return run(tile_density, tile_dest, tile_place, psf_spectrum)
+
     return jax.shard_map(
-        on_device, mesh=mesh, in_specs=in_specs, out_specs=out_specs, check_vma=False
-    )
+        local, mesh=mesh, in_specs=in_specs, out_specs=out_specs, check_vma=False
+    )

time: 120 us -> 44.2 us (0.37)
  waiting for transfers between devices: 57.2 us -> 0 us
  Pallas kernels: 0 us -> 36.2 us
  starting transfers between devices: 25 us -> 0 us
  other arithmetic: 17.2 us -> 0 us
  local copies, waits for them, and re-layouts: 14.7 us -> 7.27 us
  matrix products: 4.97 us -> 0 us
    all_to_all x6 -> x0, waiting for transfers between devices: 57.2 us -> none  [the longest x1 20.5 us: on_device(): lax.all_to_all(outgoing, 'rows', split_axis=0, concat_axis=0, tiled=True)]
    pallas_call x0 -> x2, Pallas kernels: none -> 36.2 us  [the longest x1 34.6 us: on_device_kernels(): pl.pallas_call(functools.partial(exchange_kernel, rows_n, cols_n, tile_si...]
    all_to_all x6 -> x0, starting transfers between devices: 25 us -> none  [the longest x1 7.25 us: on_device(): lax.all_to_all(labels, 'rows', split_axis=0, concat_axis=0, tiled=True)]
    another operation x14 -> x0, other arithmetic: 11.7 us -> none
    another operation x9 -> x0, local copies, waits for them, and re-layouts: 5.45 us -> none  [the longest x3 2.33 us: make_table(): return jnp.stack([upper_rows, bottom], 0).astype(jnp.bfloat16)]
    dot_general x7 -> x0, matrix products: 4.97 us -> none  [the longest x1 1.52 us: on_device(): jnp.einsum('ts,tc->sc', chosen.astype(jnp.bfloat16), tiles_flat, preferre...]
    unnamed x7 -> x14, local copies, waits for them, and re-layouts: 2.15 us -> 5.21 us
    unnamed x1 -> x0, other arithmetic: 2.21 us -> none
  transfers between devices with their start and end apart: 6 -> 0, of which waited for: 6 -> 0; matrix products, arithmetic and copies ran while one was open for 15% -> 0% of each run, Pallas kernels for 0% -> 0%
where the time goes in v1:
time: 44.2 us; the launch traced here: 43.5 us
  Pallas kernels  36.2 us (82%)
  local copies, waits for them, and re-layouts  7.27 us (16%)
    pallas_call x1, Pallas kernels, on_device_kernels(): pl.pallas_call(functools.partial(exchange_kernel, rows_n, cols_n, tile_si...  34.6 us
    unnamed x14, local copies, waits for them, and re-layouts  5.21 us
    reshape x1, local copies, waits for them, and re-layouts, on_device_kernels(): tile_density.reshape(tile_count, tile_side * tile_side)  2.06 us
    pallas_call x1, Pallas kernels, on_device_kernels(): pl.pallas_call(final_kernel, out_shape=jax.ShapeDtypeStruct((rows_dev, 2,...  1.54 us

profile of v1, /device:TPU:0, one launch (start us, length us, event | category | flops | bytes accessed | tf_op | source)
XLA Modules:
  0.0 43.5 jit_solution(17506775864174306382)
XLA Ops:
  0.0 2.1 %reshape.12.x_ref = bf16[64,4096]{1,0:T(8,128)(2,1)S(1)} reshape(bf16[64,64,64]{2,1,0:T(8,128)(2,1)} %param.8) | data formatting | bytes 1048576 | tf_op jit(solution)/shard_map/reshape | solution.py:423
  2.1 0.0 copy-start
  2.1 1.6 %copy-done = bf16[8,2,256,256]{3,2,1,0:T(8,128)(2,1)S(1)} copy-done((bf16[8,2,256,256]{3,2,1,0:T(8,128)(2,1)S(1)}, bf16[8,2,256,256]{3,2,1,0:T(8,128)(2,1)}, u32[]{:S(2)}) %copy-start) | copy-done | bytes 2097176
  3.7 0.0 copy-start.1
  3.7 1.6 %copy-done.1 = bf16[1024,1024]{1,0:T(8,128)(2,1)S(1)} copy-done((bf16[1024,1024]{1,0:T(8,128)(2,1)S(1)}, bf16[1024,1024]{1,0:T(8,128)(2,1)}, u32[]{:S(2)}) %copy-start.1) | copy-done | bytes 2097176
  5.3 0.0 copy-start.4
  5.3 0.7 %copy-done.4 = f32[4,2,512]{2,1,0:T(2,128)S(1)} copy-done((f32[4,2,512]{2,1,0:T(2,128)S(1)}, f32[4,2,512]{2,1,0:T(2,128)}, u32[]{:S(2)}) %copy-start.4) | copy-done | bytes 16408
  6.0 0.0 copy-start.5
  6.0 0.7 %copy-done.5 = s32[64,1]{0,1:T(1,128)S(1)} copy-done((s32[64,1]{0,1:T(1,128)S(1)}, s32[64,1]{0,1:T(1,128)}, u32[]{:S(2)}) %copy-start.5) | copy-done | bytes 280
  6.6 0.0 copy-start.6
  6.6 0.7 %copy-done.6 = s32[64]{0:T(128)S(1)} copy-done((s32[64]{0:T(128)S(1)}, s32[64]{0:T(128)}, u32[]{:S(2)}) %copy-start.6) | copy-done | bytes 280
  7.3 0.0 copy-start.2
  7.3 0.0 copy-start.3
  7.3 34.6 %shard_map.82 = bf16[2,8,32,512]{3,2,1,0:T(8,128)(2,1)S(1)} custom-call(bf16[64,4096]{1,0:T(8,128)(2,1)S(1)} %reshape.12.x_ref, s32[1,64]{1,0:T(1,128)S(1)} %bitcast.4, s32[1,64]{1,0:T(1,128)S(1)} %bitcast.5, f32[4,2,512]{2,1,0:T(2,128)S(1)} %copy-done.4, bf16[1024,1024]{1,0:T(8,128)(2,1)S(1)} %copy-done.1, bf16[8,2,256,256]{3,2,1,0:T(8,128)(2,1)S(1)} %copy-done), custom_call_target="tpu_custom_call" | custom-call | tf_op jit(solution)/shard_map/pallas_call | solution.py:397
  41.9 0.0 copy-done.2
  42.0 0.0 copy-done.3
  42.0 1.5 %shard_map.83 = f32[256,2,512]{2,1,0:T(2,128)} custom-call(bf16[512,512]{1,0:T(8,128)(2,1)S(1)} %copy-done.2, bf16[512,512]{1,0:T(8,128)(2,1)S(1)} %bitcast.3, bf16[256,512]{1,0:T(8,128)(2,1)S(1)} %copy-done.3), custom_call_target="tpu_custom_call" | custom-call | tf_op jit(solution)/shard_map/pallas_call | solution.py:430
Async XLA Ops:
  2.1 1.6 %copy-start = (bf16[8,2,256,256]{3,2,1,0:T(8,128)(2,1)S(1)}, bf16[8,2,256,256]{3,2,1,0:T(8,128)(2,1)}, u32[]{:S(2)}) copy-start(bf16[8,2,256,256]{3,2,1,0:T(8,128)(2,1)} %constant.10.clone.mix_hbm) | copy-start | bytes 6291460
  3.7 1.6 %copy-start.1 = (bf16[1024,1024]{1,0:T(8,128)(2,1)S(1)}, bf16[1024,1024]{1,0:T(8,128)(2,1)}, u32[]{:S(2)}) copy-start(bf16[1024,1024]{1,0:T(8,128)(2,1)} %constant.8.clone.table_hbm) | copy-start | bytes 6291460
  5.3 0.7 %copy-start.4 = (f32[4,2,512]{2,1,0:T(2,128)S(1)}, f32[4,2,512]{2,1,0:T(2,128)}, u32[]{:S(2)}) copy-start(f32[4,2,512]{2,1,0:T(2,128)} %constant.9.clone.twiddle_ref) | copy-start | bytes 49156
  6.0 0.7 %copy-start.5 = (s32[64,1]{0,1:T(1,128)S(1)}, s32[64,1]{0,1:T(1,128)}, u32[]{:S(2)}) copy-start(s32[64,1]{0,1:T(1,128)} %param.9) | copy-start | bytes 772
  6.6 0.7 %copy-start.6 = (s32[64]{0:T(128)S(1)}, s32[64]{0:T(128)}, u32[]{:S(2)}) copy-start(s32[64]{0:T(128)} %param.10) | copy-start | bytes 772
  7.3 34.7 %copy-start.2 = (bf16[512,512]{1,0:T(8,128)(2,1)S(1)}, bf16[512,512]{1,0:T(8,128)(2,1)}, u32[]{:S(2)}) copy-start(bf16[512,512]{1,0:T(8,128)(2,1)} %constant.11.clone.final_ref) | copy-start | bytes 1572868
  7.3 34.7 %copy-start.3 = (bf16[256,512]{1,0:T(8,128)(2,1)S(1)}, bf16[256,512]{1,0:T(8,128)(2,1)}, u32[]{:S(2)}) copy-start(bf16[256,512]{1,0:T(8,128)(2,1)} %psf_ref.1) | copy-start | bytes 786436

commit v2 on v1

--- a/solution.py
+++ b/solution.py
@@ -137,6 +137,7 @@
         and cols_dev % 128 == 0
         and rows_dev % tile_side == 0
         and (tile_side // rows_n // CHUNKS) * (rows_dev // tile_side) % 16 == 0
+        and 2 * cols_dev % (2 * tile_side // CHUNKS * (rows_dev // tile_side)) == 0
         and rows_n * rows_dev * cols_dev * 2 <= 1 << 22
     )
 
@@ -154,9 +155,14 @@
     f = np.arange(cols_dev)
     re, im = parts((f[:, None] * f[None, :] % cols_dev) / cols_dev, 1.0 / math.sqrt(slab_cols))
     row_table = np.block([[re, im], [-im, re]])
+    bf16 = jnp.bfloat16
     k = np.arange(cols_n)
     re, im = parts((f[None, :] * k[:, None] % slab_cols) / slab_cols, 1.0)
-    twiddles = np.stack([re, -im], 1).astype(np.float32)
+    pair = np.concatenate([re, -im], 1)
+    upper = pair.astype(bf16).astype(np.float64)
+    extra = np.zeros((16, 2 * cols_dev))
+    extra[: 2 * cols_n] = np.stack([upper, pair - upper], 1).reshape(2 * cols_n, -1)
+    row_table = np.concatenate([row_table, extra], 0)
     b = (
         tile_side * np.arange(bands)[None, None, None, :]
         + band_rows * np.arange(rows_n)[:, None, None, None]
@@ -183,20 +189,18 @@
     final = np.stack(
         [np.concatenate([re, -im], 3), np.concatenate([im, re], 3)], 0
     ).reshape(2 * rows_dev, 2 * rows_dev)
-    return (
-        jnp.asarray(row_table.astype(jnp.bfloat16)),
-        jnp.asarray(twiddles),
-        jnp.asarray(mix.astype(jnp.bfloat16)),
-        jnp.asarray(final.astype(jnp.bfloat16)),
-    )
+    lanes = mix.shape[-1]
+    blocks = [row_table[:, at : at + lanes] for at in range(0, row_table.shape[1], lanes)]
+    tables = np.concatenate(blocks + [mix.reshape(-1, lanes)], 0)
+    return jnp.asarray(tables.astype(bf16)), jnp.asarray(final.astype(bf16))
 
 
 def exchange_kernel(
     rows_n, cols_n, tile_side, bands, per_row,
-    x_ref, dest_ref, place_ref, twiddle_ref, table_hbm, mix_hbm,
+    x_ref, dest_hbm, place_hbm, tables_hbm,
     out_ref,
-    labels, arrived, dense, outgoing, table, mix,
-    label_send, label_recv, a_send, a_recv, g_send, g_recv, e_send, e_recv, local_sem,
+    owned, labels, arrived, dense, outgoing, table, mix,
+    label_send, label_recv, a_send, a_recv, g_send, g_recv, e_send, e_recv, local_sem, table_sem,
 ):
     me_row, me_col = lax.axis_index("rows"), lax.axis_index("cols")
     tiles = x_ref.shape[0]
@@ -213,8 +217,31 @@
     for d in range(1, cols_n):
         pl.semaphore_signal(barrier, inc=1, device_id=(me_row, col_peers[d]), device_id_type=MESH)
 
-    place = place_ref[...]
-    code = (place % per_row) * (rows_n * bands) + dest_ref[...] * bands + place // per_row
+    owned_copies = [
+        pltpu.make_async_copy(dest_hbm, owned.at[0], local_sem.at[2 * CHUNKS + 2]),
+        pltpu.make_async_copy(place_hbm, owned.at[1], local_sem.at[2 * CHUNKS + 3]),
+    ]
+    table_rows, lanes = table.shape[0], mix.shape[1]
+    table_copies = [
+        pltpu.make_async_copy(
+            tables_hbm.at[pl.ds(j * table_rows, table_rows), :],
+            table.at[:, pl.ds(j * lanes, lanes)],
+            table_sem.at[j],
+        )
+        for j in range(table.shape[1] // lanes)
+    ]
+    mix_start = table_rows * len(table_copies) + me_row * mix.shape[0]
+    mix_copy = pltpu.make_async_copy(
+        tables_hbm.at[pl.ds(pl.multiple_of(mix_start, 16), mix.shape[0]), :],
+        mix,
+        local_sem.at[CHUNKS],
+    )
+    for copy in owned_copies + table_copies + [mix_copy]:
+        copy.start()
+    for copy in owned_copies:
+        copy.wait()
+    slab, place = owned[0], owned[1]
+    code = (place % per_row) * (rows_n * bands) + slab * bands + place // per_row
     labels[0] = jnp.broadcast_to(
         jnp.concatenate([code, jnp.zeros((1, 128 - tiles), jnp.int32)], 1)
         if tiles < 128
@@ -256,9 +283,7 @@
                 x_ref.at[:, pl.ds(start, chunk)], arrived.at[h, 0], local_sem.at[h]
             )
         )
-    table_copy = pltpu.make_async_copy(table_hbm, table, local_sem.at[CHUNKS])
-    mix_copy = pltpu.make_async_copy(mix_hbm.at[me_row], mix, local_sem.at[CHUNKS + 1])
-    for copy in own_copies + [table_copy, mix_copy]:
+    for copy in own_copies:
         copy.start()
 
     for copy in label_copies:
@@ -309,10 +334,14 @@
             copy.start()
         gathers.append(group)
 
-    cosine = twiddle_ref[me_col, 0:1, :]
-    sine = twiddle_ref[me_col, 1:2, :]
-    table_copy.wait()
+    for copy in table_copies:
+        copy.wait()
     mix_copy.wait()
+    terms = table[2 * cols_dev :, :].astype(jnp.float32)
+    row = lax.broadcasted_iota(jnp.int32, terms.shape, 0)
+    twiddle_pair = jnp.sum(jnp.where(row // 2 == me_col, terms, 0.0), axis=0, keepdims=True)
+    mix_rows = mix.shape[0] // CHUNKS
+    cosine, sine = twiddle_pair[:, :cols_dev], twiddle_pair[:, cols_dev:]
     sends = []
     for h in range(CHUNKS):
         for copy in gathers[h]:
@@ -329,10 +358,12 @@
         section_one = jnp.concatenate(
             [sum_real * cosine + sum_imag * sine, sum_imag * cosine - sum_real * sine], 1
         ).astype(jnp.bfloat16)
-        spectrum = jnp.dot(section_one, table[...], preferred_element_type=jnp.float32)
+        spectrum = jnp.dot(section_one, table[0 : 2 * cols_dev, :], preferred_element_type=jnp.float32)
         spectrum = spectrum.astype(jnp.bfloat16)
         stacked = jnp.concatenate([spectrum[:, :cols_dev], spectrum[:, cols_dev:]], 0)
-        section_two = jnp.dot(mix[h], stacked, preferred_element_type=jnp.float32)
+        section_two = jnp.dot(
+            mix[h * mix_rows : (h + 1) * mix_rows, :], stacked, preferred_element_type=jnp.float32
+        )
         outgoing[h] = section_two.astype(jnp.bfloat16).reshape(outgoing.shape[1:])
         group = [
             pltpu.make_async_remote_copy(
@@ -388,24 +419,26 @@
     bands, per_row = rows_dev // tile_side, cols_dev // tile_side
     step_rows = tile_side // rows_n // CHUNKS
     chunk = step_rows * tile_side
-    row_table, twiddles, mix, final = constants(rows_n, cols_n, tile_side, rows_dev, cols_dev)
+    tables, final = constants(rows_n, cols_n, tile_side, rows_dev, cols_dev)
     bf16 = jnp.bfloat16
     vmem = pl.BlockSpec(memory_space=pltpu.VMEM)
     anywhere = pl.BlockSpec(memory_space=pl.ANY)
     width = 2 * step_rows * bands
+    mix_side = width * rows_n
     dma = pltpu.SemaphoreType.DMA
     section = pl.pallas_call(
         functools.partial(exchange_kernel, rows_n, cols_n, tile_side, bands, per_row),
         out_shape=jax.ShapeDtypeStruct((CHUNKS, rows_n, width, cols_dev), bf16),
-        in_specs=[vmem, vmem, vmem, vmem, anywhere, anywhere],
+        in_specs=[anywhere] * 4,
         out_specs=vmem,
         scratch_shapes=[
+            pltpu.VMEM((2, 1, tile_count), jnp.int32),
             pltpu.VMEM((rows_n, 8, 128), jnp.int32),
             pltpu.VMEM((CHUNKS, rows_n, tile_count, chunk), bf16),
             pltpu.VMEM((CHUNKS, cols_n, step_rows * rows_n * bands, cols_dev), bf16),
             pltpu.VMEM((CHUNKS, rows_n, width, cols_dev), bf16),
-            pltpu.VMEM(row_table.shape, bf16),
-            pltpu.VMEM(mix.shape[1:], bf16),
+            pltpu.VMEM((2 * cols_dev + 16, 2 * cols_dev), bf16),
+            pltpu.VMEM((CHUNKS * mix_side, mix_side), bf16),
             dma((rows_n,)),
             dma((rows_n,)),
             dma((CHUNKS, rows_n)),
@@ -414,18 +447,17 @@
             dma((CHUNKS, cols_n)),
             dma((CHUNKS, rows_n)),
             dma((CHUNKS, rows_n)),
-            dma((2 * CHUNKS + 2,)),
+            dma((2 * CHUNKS + 4,)),
+            dma((2 * cols_dev // mix_side,)),
         ],
         compiler_params=pltpu.CompilerParams(
-            collective_id=0, has_side_effects=True, vmem_limit_bytes=48 << 20
+            collective_id=0, has_side_effects=True, vmem_limit_bytes=58 << 20
         ),
     )(
         tile_density.reshape(tile_count, tile_side * tile_side),
         tile_dest.reshape(1, tile_count),
         tile_place.reshape(1, tile_count),
-        twiddles,
-        row_table,
-        mix,
+        tables,
     )
     return pl.pallas_call(
         final_kernel,

time: 44.2 us -> 41.4 us (0.937)
  local copies, waits for them, and re-layouts: 7.27 us -> 3.82 us
  Pallas kernels: 36.2 us -> 37 us
    unnamed x14 -> x6, local copies, waits for them, and re-layouts: 5.21 us -> 1.04 us
    pallas_call x1, Pallas kernels: 34.6 us -> 35.5 us  [on_device_kernels(): pl.pallas_call(functools.partial(exchange_kernel, rows_n, cols_n, tile_si...]
    reshape x1, local copies, waits for them, and re-layouts: 2.06 us -> 2.78 us  [on_device_kernels(): tile_density.reshape(tile_count, tile_side * tile_side)]
where the time goes in v2:
time: 41.4 us; the launch traced here: 40.9 us
  Pallas kernels  37 us (89%)
  local copies, waits for them, and re-layouts  3.82 us (9%)
    pallas_call x1, Pallas kernels, on_device_kernels(): pl.pallas_call(functools.partial(exchange_kernel, rows_n, cols_n, tile_si...  35.5 us
    reshape x1, local copies, waits for them, and re-layouts, on_device_kernels(): tile_density.reshape(tile_count, tile_side * tile_side)  2.78 us
    pallas_call x1, Pallas kernels, on_device_kernels(): pl.pallas_call(final_kernel, out_shape=jax.ShapeDtypeStruct((rows_dev, 2,...  1.54 us
    unnamed x6, local copies, waits for them, and re-layouts  1.04 us

profile of v2, /device:TPU:0, one launch (start us, length us, event | category | flops | bytes accessed | tf_op | source)
XLA Modules:
  0.0 40.9 jit_solution(10396061144654638235)
XLA Ops:
  0.0 0.0 copy-start.1
  0.0 0.0 copy-start.2
  0.0 2.8 %reshape.12.x_ref = bf16[64,4096]{1,0:T(8,128)(2,1)} reshape(bf16[64,64,64]{2,1,0:T(8,128)(2,1)} %param.6) | data formatting | bytes 1048576 | tf_op jit(solution)/shard_map/reshape | solution.py:457
  2.8 35.5 %shard_map.64 = bf16[2,8,32,512]{3,2,1,0:T(8,128)(2,1)} custom-call(bf16[64,4096]{1,0:T(8,128)(2,1)} %reshape.12.x_ref, s32[1,64]{1,0:T(1,128)} %bitcast.4, s32[1,64]{1,0:T(1,128)} %bitcast.5, bf16[8256,256]{1,0:T(8,128)(2,1)} %constant.4.clone.tables_hbm), custom_call_target="tpu_custom_call" | custom-call | tf_op jit(solution)/shard_map/pallas_call | solution.py:429
  38.3 0.0 copy-done.1
  38.3 0.0 copy-done.2
  38.3 0.0 copy-start
  38.3 1.0 %copy-done = bf16[2,8,32,512]{3,2,1,0:T(8,128)(2,1)S(1)} copy-done((bf16[2,8,32,512]{3,2,1,0:T(8,128)(2,1)S(1)}, bf16[2,8,32,512]{3,2,1,0:T(8,128)(2,1)}, u32[]{:S(2)}) %copy-start) | copy-done | bytes 524312
  39.3 1.5 %shard_map.65 = f32[256,2,512]{2,1,0:T(2,128)} custom-call(bf16[512,512]{1,0:T(8,128)(2,1)S(1)} %copy-done.1, bf16[512,512]{1,0:T(8,128)(2,1)S(1)} %bitcast.3, bf16[256,512]{1,0:T(8,128)(2,1)S(1)} %copy-done.2), custom_call_target="tpu_custom_call" | custom-call | tf_op jit(solution)/shard_map/pallas_call | solution.py:462
Async XLA Ops:
  0.0 38.3 %copy-start.1 = (bf16[512,512]{1,0:T(8,128)(2,1)S(1)}, bf16[512,512]{1,0:T(8,128)(2,1)}, u32[]{:S(2)}) copy-start(bf16[512,512]{1,0:T(8,128)(2,1)} %constant.5.clone.final_ref) | copy-start | bytes 1572868
  0.0 38.3 %copy-start.2 = (bf16[256,512]{1,0:T(8,128)(2,1)S(1)}, bf16[256,512]{1,0:T(8,128)(2,1)}, u32[]{:S(2)}) copy-start(bf16[256,512]{1,0:T(8,128)(2,1)} %psf_ref.1) | copy-start | bytes 786436
  38.3 1.0 %copy-start = (bf16[2,8,32,512]{3,2,1,0:T(8,128)(2,1)S(1)}, bf16[2,8,32,512]{3,2,1,0:T(8,128)(2,1)}, u32[]{:S(2)}) copy-start(bf16[2,8,32,512]{3,2,1,0:T(8,128)(2,1)} %shard_map.64) | copy-start | bytes 1572868

commit v3 on v2

--- a/solution.py
+++ b/solution.py
@@ -122,7 +122,8 @@
     return result_spec * psf_spectrum.astype(jnp.float32)[:, None, :]
 
 
-CHUNKS = 2
+CHUNKS = 4
+TABLE_LANES = 256
 MESH = pl.DeviceIdType.MESH
 
 
@@ -136,8 +137,9 @@
         and tile_count <= 128
         and cols_dev % 128 == 0
         and rows_dev % tile_side == 0
-        and (tile_side // rows_n // CHUNKS) * (rows_dev // tile_side) % 16 == 0
-        and 2 * cols_dev % (2 * tile_side // CHUNKS * (rows_dev // tile_side)) == 0
+        and 2 * (tile_side // rows_n // CHUNKS) * (rows_dev // tile_side) % 16 == 0
+        and 2 * tile_side // CHUNKS * (rows_dev // tile_side) <= TABLE_LANES
+        and 2 * cols_dev % TABLE_LANES == 0
         and rows_n * rows_dev * cols_dev * 2 <= 1 << 22
     )
 
@@ -189,9 +191,10 @@
     final = np.stack(
         [np.concatenate([re, -im], 3), np.concatenate([im, re], 3)], 0
     ).reshape(2 * rows_dev, 2 * rows_dev)
-    lanes = mix.shape[-1]
+    lanes = TABLE_LANES
+    mix = np.pad(mix.reshape(-1, mix.shape[-1]), ((0, 0), (0, lanes - mix.shape[-1])))
     blocks = [row_table[:, at : at + lanes] for at in range(0, row_table.shape[1], lanes)]
-    tables = np.concatenate(blocks + [mix.reshape(-1, lanes)], 0)
+    tables = np.concatenate(blocks + [mix], 0)
     return jnp.asarray(tables.astype(bf16)), jnp.asarray(final.astype(bf16))
 
 
@@ -221,7 +224,7 @@
         pltpu.make_async_copy(dest_hbm, owned.at[0], local_sem.at[2 * CHUNKS + 2]),
         pltpu.make_async_copy(place_hbm, owned.at[1], local_sem.at[2 * CHUNKS + 3]),
     ]
-    table_rows, lanes = table.shape[0], mix.shape[1]
+    table_rows, lanes = table.shape[0], TABLE_LANES
     table_copies = [
         pltpu.make_async_copy(
             tables_hbm.at[pl.ds(j * table_rows, table_rows), :],
@@ -232,7 +235,7 @@
     ]
     mix_start = table_rows * len(table_copies) + me_row * mix.shape[0]
     mix_copy = pltpu.make_async_copy(
-        tables_hbm.at[pl.ds(pl.multiple_of(mix_start, 16), mix.shape[0]), :],
+        tables_hbm.at[pl.ds(pl.multiple_of(mix_start, 16), mix.shape[0]), pl.ds(0, mix.shape[1])],
         mix,
         local_sem.at[CHUNKS],
     )
@@ -295,8 +298,17 @@
     ).astype(jnp.bfloat16)
     low_lanes = lax.broadcasted_iota(jnp.int32, (rows_n * bands, 128), 1) < tile_side
 
+    for copy in table_copies + [mix_copy]:
+        copy.wait()
+    terms = table[2 * cols_dev :, :].astype(jnp.float32)
+    row = lax.broadcasted_iota(jnp.int32, terms.shape, 0)
+    twiddle_pair = jnp.sum(jnp.where(row // 2 == me_col, terms, 0.0), axis=0, keepdims=True)
+    mix_rows = mix.shape[0] // CHUNKS
+    cosine, sine = twiddle_pair[:, :cols_dev], twiddle_pair[:, cols_dev:]
+
     gathers = []
-    for h in range(CHUNKS):
+
+    def density_stage(h):
         own_copies[h].wait()
         for copy in band_copies[h]:
             copy.wait_recv()
@@ -334,16 +346,9 @@
             copy.start()
         gathers.append(group)
 
-    for copy in table_copies:
-        copy.wait()
-    mix_copy.wait()
-    terms = table[2 * cols_dev :, :].astype(jnp.float32)
-    row = lax.broadcasted_iota(jnp.int32, terms.shape, 0)
-    twiddle_pair = jnp.sum(jnp.where(row // 2 == me_col, terms, 0.0), axis=0, keepdims=True)
-    mix_rows = mix.shape[0] // CHUNKS
-    cosine, sine = twiddle_pair[:, :cols_dev], twiddle_pair[:, cols_dev:]
     sends = []
-    for h in range(CHUNKS):
+
+    def section_stage(h):
         for copy in gathers[h]:
             copy.wait_recv()
         sum_real = sum_imag = None
@@ -383,6 +388,12 @@
         )
         own.start()
         sends.append((group, own))
+
+    for h in range(CHUNKS):
+        density_stage(h)
+        if h > 0:
+            section_stage(h - 1)
+    section_stage(CHUNKS - 1)
 
     for copy in label_copies:
         copy.wait_send()
@@ -448,10 +459,10 @@
             dma((CHUNKS, rows_n)),
             dma((CHUNKS, rows_n)),
             dma((2 * CHUNKS + 4,)),
-            dma((2 * cols_dev // mix_side,)),
+            dma((2 * cols_dev // TABLE_LANES,)),
         ],
         compiler_params=pltpu.CompilerParams(
-            collective_id=0, has_side_effects=True, vmem_limit_bytes=58 << 20
+            collective_id=0, has_side_effects=True, vmem_limit_bytes=56 << 20
         ),
     )(
         tile_density.reshape(tile_count, tile_side * tile_side),

time: 41.4 us -> 40.9 us (0.988)
  no operation moved by 1% of the time
where the time goes in v3:
time: 40.9 us; the launch traced here: 40.7 us
  Pallas kernels  36.8 us (90%)
  local copies, waits for them, and re-layouts  3.82 us (9%)
    pallas_call x1, Pallas kernels, on_device_kernels(): pl.pallas_call(functools.partial(exchange_kernel, rows_n, cols_n, tile_si...  35.3 us
    reshape x1, local copies, waits for them, and re-layouts, on_device_kernels(): tile_density.reshape(tile_count, tile_side * tile_side)  2.78 us
    pallas_call x1, Pallas kernels, on_device_kernels(): pl.pallas_call(final_kernel, out_shape=jax.ShapeDtypeStruct((rows_dev, 2,...  1.54 us
    unnamed x6, local copies, waits for them, and re-layouts  1.04 us

profile of v3, /device:TPU:0, one launch (start us, length us, event | category | flops | bytes accessed | tf_op | source)
XLA Modules:
  0.0 40.7 jit_solution(15879087625595773863)
XLA Ops:
  0.0 0.0 copy-start.1
  0.0 0.0 copy-start.2
  0.0 2.8 %reshape.12.x_ref = bf16[64,4096]{1,0:T(8,128)(2,1)} reshape(bf16[64,64,64]{2,1,0:T(8,128)(2,1)} %param.6) | data formatting | bytes 1048576 | tf_op jit(solution)/shard_map/reshape | solution.py:468
  2.8 35.3 %shard_map.64 = bf16[4,8,16,512]{3,2,1,0:T(8,128)(2,1)} custom-call(bf16[64,4096]{1,0:T(8,128)(2,1)} %reshape.12.x_ref, s32[1,64]{1,0:T(1,128)} %bitcast.4, s32[1,64]{1,0:T(1,128)} %bitcast.5, bf16[8256,256]{1,0:T(8,128)(2,1)} %constant.4.clone.tables_hbm), custom_call_target="tpu_custom_call" | custom-call | tf_op jit(solution)/shard_map/pallas_call | solution.py:440
  38.1 0.0 copy-done.1
  38.1 0.0 copy-done.2
  38.1 0.0 copy-start
  38.1 1.0 %copy-done = bf16[4,8,16,512]{3,2,1,0:T(8,128)(2,1)S(1)} copy-done((bf16[4,8,16,512]{3,2,1,0:T(8,128)(2,1)S(1)}, bf16[4,8,16,512]{3,2,1,0:T(8,128)(2,1)}, u32[]{:S(2)}) %copy-start) | copy-done | bytes 524312
  39.2 1.5 %shard_map.65 = f32[256,2,512]{2,1,0:T(2,128)} custom-call(bf16[512,512]{1,0:T(8,128)(2,1)S(1)} %copy-done.1, bf16[512,512]{1,0:T(8,128)(2,1)S(1)} %bitcast.3, bf16[256,512]{1,0:T(8,128)(2,1)S(1)} %copy-done.2), custom_call_target="tpu_custom_call" | custom-call | tf_op jit(solution)/shard_map/pallas_call | solution.py:473
Async XLA Ops:
  0.0 38.1 %copy-start.1 = (bf16[512,512]{1,0:T(8,128)(2,1)S(1)}, bf16[512,512]{1,0:T(8,128)(2,1)}, u32[]{:S(2)}) copy-start(bf16[512,512]{1,0:T(8,128)(2,1)} %constant.5.clone.final_ref) | copy-start | bytes 1572868
  0.0 38.1 %copy-start.2 = (bf16[256,512]{1,0:T(8,128)(2,1)S(1)}, bf16[256,512]{1,0:T(8,128)(2,1)}, u32[]{:S(2)}) copy-start(bf16[256,512]{1,0:T(8,128)(2,1)} %psf_ref.1) | copy-start | bytes 786436
  38.1 1.0 %copy-start = (bf16[4,8,16,512]{3,2,1,0:T(8,128)(2,1)S(1)}, bf16[4,8,16,512]{3,2,1,0:T(8,128)(2,1)}, u32[]{:S(2)}) copy-start(bf16[4,8,16,512]{3,2,1,0:T(8,128)(2,1)} %shard_map.64) | copy-start | bytes 1572868

commit v4 on v3

--- a/solution.py
+++ b/solution.py
@@ -200,26 +200,28 @@
 
 def exchange_kernel(
     rows_n, cols_n, tile_side, bands, per_row,
-    x_ref, dest_hbm, place_hbm, tables_hbm,
+    tiles_hbm, dest_hbm, place_hbm, tables_hbm,
     out_ref,
-    owned, labels, arrived, dense, outgoing, table, mix,
+    owned, raw, wide, banded, labels, arrived, dense, outgoing, table, mix,
     label_send, label_recv, a_send, a_recv, g_send, g_recv, e_send, e_recv, local_sem, table_sem,
 ):
     me_row, me_col = lax.axis_index("rows"), lax.axis_index("cols")
-    tiles = x_ref.shape[0]
+    tiles = tiles_hbm.shape[0]
     chunk = arrived.shape[3]
-    band = chunk * CHUNKS
     cols_dev = per_row * tile_side
     row_peers = [lax.rem(me_row + d, rows_n) for d in range(rows_n)]
     row_sources = [lax.rem(me_row + rows_n - d, rows_n) for d in range(rows_n)]
-    col_peers = [lax.rem(me_col + d, cols_n) for d in range(cols_n)]
+    sibling = me_col + 1 - 2 * lax.rem(me_col, 2)
+    col_blocks = [me_col, sibling, lax.rem(me_col + 2, cols_n), lax.rem(sibling + 2, cols_n)]
 
     barrier = pltpu.get_barrier_semaphore()
     for d in range(1, rows_n):
         pl.semaphore_signal(barrier, inc=1, device_id=(row_peers[d], me_col), device_id_type=MESH)
-    for d in range(1, cols_n):
-        pl.semaphore_signal(barrier, inc=1, device_id=(me_row, col_peers[d]), device_id_type=MESH)
-
+    for d in range(1, 3):
+        pl.semaphore_signal(barrier, inc=1, device_id=(me_row, col_blocks[d]), device_id_type=MESH)
+
+    raw_copy = pltpu.make_async_copy(tiles_hbm, raw, local_sem.at[CHUNKS + 1])
+    raw_copy.start()
     owned_copies = [
         pltpu.make_async_copy(dest_hbm, owned.at[0], local_sem.at[2 * CHUNKS + 2]),
         pltpu.make_async_copy(place_hbm, owned.at[1], local_sem.at[2 * CHUNKS + 3]),
@@ -251,12 +253,30 @@
         else code,
         labels.shape[1:],
     )
-    pl.semaphore_wait(barrier, rows_n + cols_n - 2)
+    low_lanes = lax.broadcasted_iota(jnp.int32, (max(tiles, rows_n * bands), 128), 1) < tile_side
+    raw_copy.wait()
+    wide[:, 0:tile_side] = raw[...].reshape(tiles * tile_side, tile_side).astype(jnp.float32)
+    own_copies = [
+        pltpu.make_async_copy(banded.at[h, me_row], arrived.at[h, 0], local_sem.at[h])
+        for h in range(CHUNKS)
+    ]
+
+    def band_stage(h):
+        for owner in range(rows_n):
+            for pair in range(chunk // 128):
+                row = (owner * CHUNKS + h) * (chunk // tile_side) + 2 * pair
+                first = wide[pl.ds(row, tiles, stride=tile_side), :]
+                second = wide[pl.ds(row + 1, tiles, stride=tile_side), :]
+                both = jnp.where(low_lanes[:tiles], first, pltpu.roll(second, tile_side, 1))
+                banded[h, owner, :, 128 * pair : 128 * pair + 128] = both.astype(jnp.bfloat16)
+        own_copies[h].start()
+
+    band_stage(0)
+    pl.semaphore_wait(barrier, rows_n + 1)
 
     def band_copy(h, d):
-        start = pl.multiple_of(row_peers[d] * band + h * chunk, 128)
         return pltpu.make_async_remote_copy(
-            src_ref=x_ref.at[:, pl.ds(start, chunk)],
+            src_ref=banded.at[h, row_peers[d]],
             dst_ref=arrived.at[h, d],
             send_sem=a_send.at[h, d],
             recv_sem=a_recv.at[h, d],
@@ -276,18 +296,16 @@
         for d in range(1, rows_n)
     ]
     band_copies = [[band_copy(h, d) for d in range(1, rows_n)] for h in range(CHUNKS)]
-    for copy in label_copies + [copy for group in band_copies for copy in group]:
+    for copy in label_copies:
         copy.start()
-    own_copies = []
-    for h in range(CHUNKS):
-        start = pl.multiple_of(me_row * band + h * chunk, 128)
-        own_copies.append(
-            pltpu.make_async_copy(
-                x_ref.at[:, pl.ds(start, chunk)], arrived.at[h, 0], local_sem.at[h]
-            )
-        )
-    for copy in own_copies:
-        copy.start()
+    def band_start(h):
+        for copy in band_copies[h]:
+            copy.start()
+
+    band_start(0)
+    for h in range(1, CHUNKS):
+        band_stage(h)
+    band_start(1)
 
     for copy in label_copies:
         copy.wait_recv()
@@ -296,7 +314,6 @@
     hot = jnp.where(
         lax.broadcasted_iota(jnp.int32, (cells, rows_n * tiles), 0) == codes, 1.0, 0.0
     ).astype(jnp.bfloat16)
-    low_lanes = lax.broadcasted_iota(jnp.int32, (rows_n * bands, 128), 1) < tile_side
 
     for copy in table_copies + [mix_copy]:
         copy.wait()
@@ -308,10 +325,22 @@
 
     gathers = []
 
+    def block_copy(h, source, peer, slot):
+        return pltpu.make_async_remote_copy(
+            src_ref=dense.at[h, source],
+            dst_ref=dense.at[h, slot],
+            send_sem=g_send.at[h, slot],
+            recv_sem=g_recv.at[h, slot],
+            device_id=(me_row, col_blocks[peer]),
+            device_id_type=MESH,
+        )
+
     def density_stage(h):
         own_copies[h].wait()
         for copy in band_copies[h]:
             copy.wait_recv()
+        if h + 2 < CHUNKS:
+            band_start(h + 2)
         summed = jnp.dot(
             hot,
             arrived[h].reshape(rows_n * tiles, chunk),
@@ -323,37 +352,33 @@
             for q in range(per_row // 2):
                 left = summed[2 * q * height : (2 * q + 1) * height, lanes]
                 right = summed[(2 * q + 1) * height : (2 * q + 2) * height, lanes]
-                upper = jnp.where(low_lanes, left, pltpu.roll(right, tile_side, 1))
-                lower = jnp.where(low_lanes, pltpu.roll(left, tile_side, 1), right)
+                upper = jnp.where(low_lanes[:height], left, pltpu.roll(right, tile_side, 1))
+                lower = jnp.where(low_lanes[:height], pltpu.roll(left, tile_side, 1), right)
                 out_lanes = slice(128 * q, 128 * q + 128)
                 first = 2 * pair * height
                 dense[h, 0, first : first + height, out_lanes] = upper.astype(jnp.bfloat16)
                 dense[h, 0, first + height : first + 2 * height, out_lanes] = lower.astype(
                     jnp.bfloat16
                 )
-        group = [
-            pltpu.make_async_remote_copy(
-                src_ref=dense.at[h, 0],
-                dst_ref=dense.at[h, d],
-                send_sem=g_send.at[h, d],
-                recv_sem=g_recv.at[h, d],
-                device_id=(me_row, col_peers[d]),
-                device_id_type=MESH,
-            )
-            for d in range(1, cols_n)
-        ]
+        group = [block_copy(h, 0, 2, 2), block_copy(h, 0, 1, 1)]
         for copy in group:
             copy.start()
         gathers.append(group)
 
+    def forward_stage(h):
+        gathers[h][0].wait_recv()
+        copy = block_copy(h, 2, 1, 3)
+        copy.start()
+        gathers[h].append(copy)
+
     sends = []
 
     def section_stage(h):
-        for copy in gathers[h]:
+        for copy in gathers[h][1:]:
             copy.wait_recv()
         sum_real = sum_imag = None
         for d in range(cols_n):
-            turn = lax.rem(lax.rem(me_col + cols_n - d, cols_n) * me_col, cols_n)
+            turn = lax.rem(col_blocks[d] * me_col, cols_n)
             cos_turn = jnp.where(turn == 0, 1.0, jnp.where(turn == 2, -1.0, 0.0))
             sin_turn = jnp.where(turn == 1, 1.0, jnp.where(turn == 3, -1.0, 0.0))
             value = dense[h, d].astype(jnp.float32)
@@ -392,8 +417,12 @@
     for h in range(CHUNKS):
         density_stage(h)
         if h > 0:
-            section_stage(h - 1)
-    section_stage(CHUNKS - 1)
+            forward_stage(h - 1)
+        if h > 1:
+            section_stage(h - 2)
+    forward_stage(CHUNKS - 1)
+    for h in range(CHUNKS - 2, CHUNKS):
+        section_stage(h)
 
     for copy in label_copies:
         copy.wait_send()
@@ -444,6 +473,9 @@
         out_specs=vmem,
         scratch_shapes=[
             pltpu.VMEM((2, 1, tile_count), jnp.int32),
+            pltpu.VMEM(tile_density.shape, bf16),
+            pltpu.VMEM((tile_count * tile_side, 128), jnp.float32),
+            pltpu.VMEM((CHUNKS, rows_n, tile_count, chunk), bf16),
             pltpu.VMEM((rows_n, 8, 128), jnp.int32),
             pltpu.VMEM((CHUNKS, rows_n, tile_count, chunk), bf16),
             pltpu.VMEM((CHUNKS, cols_n, step_rows * rows_n * bands, cols_dev), bf16),
@@ -465,7 +497,7 @@
             collective_id=0, has_side_effects=True, vmem_limit_bytes=56 << 20
         ),
     )(
-        tile_density.reshape(tile_count, tile_side * tile_side),
+        tile_density,
         tile_dest.reshape(1, tile_count),
         tile_place.reshape(1, tile_count),
         tables,

time: 40.9 us -> 38.8 us (0.949)
  local copies, waits for them, and re-layouts: 3.82 us -> 1.04 us
  Pallas kernels: 36.8 us -> 37.5 us
    reshape x1 -> x0, local copies, waits for them, and re-layouts: 2.78 us -> none  [on_device_kernels(): tile_density.reshape(tile_count, tile_side * tile_side)]
    pallas_call x1, Pallas kernels: 35.3 us -> 36 us  [on_device_kernels(): pl.pallas_call(functools.partial(exchange_kernel, rows_n, cols_n, tile_si...]
where the time goes in v4:
time: 38.8 us; the launch traced here: 38.6 us
  Pallas kernels  37.5 us (97%)
  local copies, waits for them, and re-layouts  1.04 us (3%)
    pallas_call x1, Pallas kernels, on_device_kernels(): pl.pallas_call(functools.partial(exchange_kernel, rows_n, cols_n, tile_si...  36 us
    pallas_call x1, Pallas kernels, on_device_kernels(): pl.pallas_call(final_kernel, out_shape=jax.ShapeDtypeStruct((rows_dev, 2,...  1.54 us
    unnamed x6, local copies, waits for them, and re-layouts  1.04 us

profile of v4, /device:TPU:0, one launch (start us, length us, event | category | flops | bytes accessed | tf_op | source)
XLA Modules:
  0.0 38.6 jit_solution(9310192361301516955)
XLA Ops:
  0.0 0.0 copy-start.1
  0.0 0.0 copy-start.2
  0.0 36.0 %shard_map.64 = bf16[4,8,16,512]{3,2,1,0:T(8,128)(2,1)} custom-call(bf16[64,64,64]{2,1,0:T(8,128)(2,1)} %tiles_hbm.1, s32[1,64]{1,0:T(1,128)} %bitcast.4, s32[1,64]{1,0:T(1,128)} %bitcast.5, bf16[8256,256]{1,0:T(8,128)(2,1)} %constant.4.clone.tables_hbm), custom_call_target="tpu_custom_call" | custom-call | tf_op jit(solution)/shard_map/pallas_call | solution.py:469
  36.0 0.0 copy-done.1
  36.0 0.0 copy-done.2
  36.0 0.0 copy-start
  36.0 1.0 %copy-done = bf16[4,8,16,512]{3,2,1,0:T(8,128)(2,1)S(1)} copy-done((bf16[4,8,16,512]{3,2,1,0:T(8,128)(2,1)S(1)}, bf16[4,8,16,512]{3,2,1,0:T(8,128)(2,1)}, u32[]{:S(2)}) %copy-start) | copy-done | bytes 524312
  37.1 1.5 %shard_map.65 = f32[256,2,512]{2,1,0:T(2,128)} custom-call(bf16[512,512]{1,0:T(8,128)(2,1)S(1)} %copy-done.1, bf16[512,512]{1,0:T(8,128)(2,1)S(1)} %bitcast.3, bf16[256,512]{1,0:T(8,128)(2,1)S(1)} %copy-done.2), custom_call_target="tpu_custom_call" | custom-call | tf_op jit(solution)/shard_map/pallas_call | solution.py:505
Async XLA Ops:
  0.0 36.0 %copy-start.1 = (bf16[512,512]{1,0:T(8,128)(2,1)S(1)}, bf16[512,512]{1,0:T(8,128)(2,1)}, u32[]{:S(2)}) copy-start(bf16[512,512]{1,0:T(8,128)(2,1)} %constant.5.clone.final_ref) | copy-start | bytes 1572868
  0.0 36.0 %copy-start.2 = (bf16[256,512]{1,0:T(8,128)(2,1)S(1)}, bf16[256,512]{1,0:T(8,128)(2,1)}, u32[]{:S(2)}) copy-start(bf16[256,512]{1,0:T(8,128)(2,1)} %psf_ref.1) | copy-start | bytes 786436
  36.0 1.0 %copy-start = (bf16[4,8,16,512]{3,2,1,0:T(8,128)(2,1)S(1)}, bf16[4,8,16,512]{3,2,1,0:T(8,128)(2,1)}, u32[]{:S(2)}) copy-start(bf16[4,8,16,512]{3,2,1,0:T(8,128)(2,1)} %shard_map.64) | copy-start | bytes 1572868

commit v5 on v4

--- a/solution.py
+++ b/solution.py
@@ -122,7 +122,7 @@
     return result_spec * psf_spectrum.astype(jnp.float32)[:, None, :]
 
 
-CHUNKS = 4
+CHUNKS = 2
 TABLE_LANES = 256
 MESH = pl.DeviceIdType.MESH
 
@@ -443,9 +443,22 @@
             ).wait()
 
 
-def final_kernel(final_ref, section_ref, psf_ref, out_ref):
+def final_kernel(final_ref, section_hbm, psf_ref, out_ref, section, sems):
     rows_dev = psf_ref.shape[0]
-    result = jnp.dot(final_ref[...], section_ref[...], preferred_element_type=jnp.float32)
+    depth = section.shape[0] // CHUNKS
+    copies = []
+    for h in range(CHUNKS):
+        rows = pl.ds(h * depth, depth)
+        copies.append(
+            pltpu.make_async_copy(section_hbm.at[rows, :], section.at[rows, :], sems.at[h])
+        )
+        copies[h].start()
+    result = None
+    for h in range(CHUNKS):
+        copies[h].wait()
+        at = slice(h * depth, h * depth + depth)
+        term = jnp.dot(final_ref[:, at], section[at, :], preferred_element_type=jnp.float32)
+        result = term if h == 0 else result + term
     psf = psf_ref[...].astype(jnp.float32)
     out_ref[:, 0, :] = result[:rows_dev] * psf
     out_ref[:, 1, :] = result[rows_dev:] * psf
@@ -505,9 +518,10 @@
     return pl.pallas_call(
         final_kernel,
         out_shape=jax.ShapeDtypeStruct((rows_dev, 2, cols_dev), jnp.float32),
-        in_specs=[vmem, vmem, vmem],
+        in_specs=[vmem, anywhere, vmem],
         out_specs=vmem,
-        compiler_params=pltpu.CompilerParams(vmem_limit_bytes=32 << 20),
+        scratch_shapes=[pltpu.VMEM((2 * rows_dev, cols_dev), bf16), dma((CHUNKS,))],
+        compiler_params=pltpu.CompilerParams(vmem_limit_bytes=56 << 20),
     )(final, section.reshape(2 * rows_dev, cols_dev), psf_spectrum)
 
 

time: 38.8 us -> 40.9 us (1.054)
  Pallas kernels: 37.5 us -> 40.5 us
  local copies, waits for them, and re-layouts: 1.04 us -> 0 us
    pallas_call x1, Pallas kernels: 1.54 us -> 3.7 us  [on_device_kernels(): pl.pallas_call(final_kernel, out_shape=jax.ShapeDtypeStruct((rows_dev, 2,...]
    unnamed x6 -> x0, local copies, waits for them, and re-layouts: 1.04 us -> none
    pallas_call x1, Pallas kernels: 36 us -> 36.8 us  [on_device_kernels(): pl.pallas_call(functools.partial(exchange_kernel, rows_n, cols_n, tile_si...]
where the time goes in v5:
time: 40.9 us; the launch traced here: 40.5 us
  Pallas kernels  40.5 us (99%)
    pallas_call x1, Pallas kernels, on_device_kernels(): pl.pallas_call(functools.partial(exchange_kernel, rows_n, cols_n, tile_si...  36.8 us
    pallas_call x1, Pallas kernels, on_device_kernels(): pl.pallas_call(final_kernel, out_shape=jax.ShapeDtypeStruct((rows_dev, 2,...  3.7 us

profile of v5, /device:TPU:0, one launch (start us, length us, event | category | flops | bytes accessed | tf_op | source)
XLA Modules:
  0.0 40.5 jit_solution(13668423946221734849)
XLA Ops:
  0.0 36.8 %shard_map.64 = bf16[2,8,32,512]{3,2,1,0:T(8,128)(2,1)} custom-call(bf16[64,64,64]{2,1,0:T(8,128)(2,1)} %tiles_hbm.1, s32[1,64]{1,0:T(1,128)} %bitcast.4, s32[1,64]{1,0:T(1,128)} %bitcast.5, bf16[8256,256]{1,0:T(8,128)(2,1)} %constant.4.clone.tables_hbm), custom_call_target="tpu_custom_call" | custom-call | tf_op jit(solution)/shard_map/pallas_call | solution.py:482
  36.8 3.7 %shard_map.65 = f32[256,2,512]{2,1,0:T(2,128)} custom-call(bf16[512,512]{1,0:T(8,128)(2,1)} %constant.5.clone.final_ref, bf16[512,512]{1,0:T(8,128)(2,1)} %bitcast.3, bf16[256,512]{1,0:T(8,128)(2,1)} %psf_ref.1), custom_call_target="tpu_custom_call" | custom-call | tf_op jit(solution)/shard_map/pallas_call | solution.py:518

commit v6 on v4

--- a/solution.py
+++ b/solution.py
@@ -305,7 +305,7 @@
     band_start(0)
     for h in range(1, CHUNKS):
         band_stage(h)
-    band_start(1)
+        band_start(h)
 
     for copy in label_copies:
         copy.wait_recv()
@@ -339,8 +339,6 @@
         own_copies[h].wait()
         for copy in band_copies[h]:
             copy.wait_recv()
-        if h + 2 < CHUNKS:
-            band_start(h + 2)
         summed = jnp.dot(
             hot,
             arrived[h].reshape(rows_n * tiles, chunk),
@@ -420,9 +418,9 @@
             forward_stage(h - 1)
         if h > 1:
             section_stage(h - 2)
+    section_stage(CHUNKS - 2)
     forward_stage(CHUNKS - 1)
-    for h in range(CHUNKS - 2, CHUNKS):
-        section_stage(h)
+    section_stage(CHUNKS - 1)
 
     for copy in label_copies:
         copy.wait_send()

time: 38.8 us -> 39.7 us (1.023)
  Pallas kernels: 37.5 us -> 38.5 us
    pallas_call x1, Pallas kernels: 36 us -> 36.9 us  [on_device_kernels(): pl.pallas_call(functools.partial(exchange_kernel, rows_n, cols_n, tile_si...]
where the time goes in v6:
time: 39.7 us; the launch traced here: 39.5 us
  Pallas kernels  38.5 us (97%)
  local copies, waits for them, and re-layouts  1.04 us (3%)
    pallas_call x1, Pallas kernels, on_device_kernels(): pl.pallas_call(functools.partial(exchange_kernel, rows_n, cols_n, tile_si...  36.9 us
    pallas_call x1, Pallas kernels, on_device_kernels(): pl.pallas_call(final_kernel, out_shape=jax.ShapeDtypeStruct((rows_dev, 2,...  1.54 us
    unnamed x6, local copies, waits for them, and re-layouts  1.04 us

profile of v6, /device:TPU:0, one launch (start us, length us, event | category | flops | bytes accessed | tf_op | source)
XLA Modules:
  0.0 39.5 jit_solution(3472025573527802030)
XLA Ops:
  0.0 0.0 copy-start.1
  0.0 0.0 copy-start.2
  0.0 36.9 %shard_map.64 = bf16[4,8,16,512]{3,2,1,0:T(8,128)(2,1)} custom-call(bf16[64,64,64]{2,1,0:T(8,128)(2,1)} %tiles_hbm.1, s32[1,64]{1,0:T(1,128)} %bitcast.4, s32[1,64]{1,0:T(1,128)} %bitcast.5, bf16[8256,256]{1,0:T(8,128)(2,1)} %constant.4.clone.tables_hbm), custom_call_target="tpu_custom_call" | custom-call | tf_op jit(solution)/shard_map/pallas_call | solution.py:467
  36.9 0.0 copy-done.1
  37.0 0.0 copy-done.2
  37.0 0.0 copy-start
  37.0 1.0 %copy-done = bf16[4,8,16,512]{3,2,1,0:T(8,128)(2,1)S(1)} copy-done((bf16[4,8,16,512]{3,2,1,0:T(8,128)(2,1)S(1)}, bf16[4,8,16,512]{3,2,1,0:T(8,128)(2,1)}, u32[]{:S(2)}) %copy-start) | copy-done | bytes 524312
  38.0 1.5 %shard_map.65 = f32[256,2,512]{2,1,0:T(2,128)} custom-call(bf16[512,512]{1,0:T(8,128)(2,1)S(1)} %copy-done.1, bf16[512,512]{1,0:T(8,128)(2,1)S(1)} %bitcast.3, bf16[256,512]{1,0:T(8,128)(2,1)S(1)} %copy-done.2), custom_call_target="tpu_custom_call" | custom-call | tf_op jit(solution)/shard_map/pallas_call | solution.py:503
Async XLA Ops:
  0.0 36.9 %copy-start.1 = (bf16[512,512]{1,0:T(8,128)(2,1)S(1)}, bf16[512,512]{1,0:T(8,128)(2,1)}, u32[]{:S(2)}) copy-start(bf16[512,512]{1,0:T(8,128)(2,1)} %constant.5.clone.final_ref) | copy-start | bytes 1572868
  0.0 37.0 %copy-start.2 = (bf16[256,512]{1,0:T(8,128)(2,1)S(1)}, bf16[256,512]{1,0:T(8,128)(2,1)}, u32[]{:S(2)}) copy-start(bf16[256,512]{1,0:T(8,128)(2,1)} %psf_ref.1) | copy-start | bytes 786436
  37.0 1.0 %copy-start = (bf16[4,8,16,512]{3,2,1,0:T(8,128)(2,1)S(1)}, bf16[4,8,16,512]{3,2,1,0:T(8,128)(2,1)}, u32[]{:S(2)}) copy-start(bf16[4,8,16,512]{3,2,1,0:T(8,128)(2,1)} %shard_map.64) | copy-start | bytes 1572868

commit v7 on v5

--- a/solution.py
+++ b/solution.py
@@ -122,8 +122,7 @@
     return result_spec * psf_spectrum.astype(jnp.float32)[:, None, :]
 
 
-CHUNKS = 2
-TABLE_LANES = 256
+CHUNKS = 4
 MESH = pl.DeviceIdType.MESH
 
 
@@ -138,8 +137,9 @@
         and cols_dev % 128 == 0
         and rows_dev % tile_side == 0
         and 2 * (tile_side // rows_n // CHUNKS) * (rows_dev // tile_side) % 16 == 0
-        and 2 * tile_side // CHUNKS * (rows_dev // tile_side) <= TABLE_LANES
-        and 2 * cols_dev % TABLE_LANES == 0
+        and 2 * tile_side * (rows_dev // tile_side) <= 2 * cols_dev
+        and 2 * tile_side // CHUNKS * (rows_dev // tile_side) % 128 == 0
+        and cols_n * cols_dev <= 2048
         and rows_n * rows_dev * cols_dev * 2 <= 1 << 22
     )
 
@@ -154,17 +154,15 @@
         angles = 2.0 * np.pi * phase
         return np.cos(angles) * factor, -np.sin(angles) * factor
 
-    f = np.arange(cols_dev)
-    re, im = parts((f[:, None] * f[None, :] % cols_dev) / cols_dev, 1.0 / math.sqrt(slab_cols))
-    row_table = np.block([[re, im], [-im, re]])
     bf16 = jnp.bfloat16
     k = np.arange(cols_n)
-    re, im = parts((f[None, :] * k[:, None] % slab_cols) / slab_cols, 1.0)
-    pair = np.concatenate([re, -im], 1)
-    upper = pair.astype(bf16).astype(np.float64)
-    extra = np.zeros((16, 2 * cols_dev))
-    extra[: 2 * cols_n] = np.stack([upper, pair - upper], 1).reshape(2 * cols_n, -1)
-    row_table = np.concatenate([row_table, extra], 0)
+    sibling = k + 1 - 2 * (k % 2)
+    held = np.stack([k, sibling, (k + 2) % cols_n, (sibling + 2) % cols_n], 1)
+    column = (held[:, :, None] * cols_dev + np.arange(cols_dev)).reshape(cols_n, slab_cols, 1)
+    frequency = k[:, None, None] + cols_n * np.arange(cols_dev)
+    waves = np.stack(parts(np.arange(slab_cols) / slab_cols, 1.0 / math.sqrt(slab_cols)), 0)
+    re, im = waves.astype(bf16)[:, column * frequency % slab_cols]
+    row_tables = np.concatenate([re, im], 2)
     b = (
         tile_side * np.arange(bands)[None, None, None, :]
         + band_rows * np.arange(rows_n)[:, None, None, None]
@@ -191,11 +189,11 @@
     final = np.stack(
         [np.concatenate([re, -im], 3), np.concatenate([im, re], 3)], 0
     ).reshape(2 * rows_dev, 2 * rows_dev)
-    lanes = TABLE_LANES
-    mix = np.pad(mix.reshape(-1, mix.shape[-1]), ((0, 0), (0, lanes - mix.shape[-1])))
-    blocks = [row_table[:, at : at + lanes] for at in range(0, row_table.shape[1], lanes)]
-    tables = np.concatenate(blocks + [mix], 0)
-    return jnp.asarray(tables.astype(bf16)), jnp.asarray(final.astype(bf16))
+    side = mix.shape[-1]
+    mix = mix.transpose(0, 2, 1, 3).reshape(rows_n * side, CHUNKS * side)
+    mix = np.pad(mix, ((0, 0), (0, 2 * cols_dev - CHUNKS * side)))
+    tables = np.concatenate([row_tables.reshape(-1, 2 * cols_dev), mix.astype(bf16)], 0)
+    return jnp.asarray(tables), jnp.asarray(final.astype(bf16))
 
 
 def exchange_kernel(
@@ -226,16 +224,14 @@
         pltpu.make_async_copy(dest_hbm, owned.at[0], local_sem.at[2 * CHUNKS + 2]),
         pltpu.make_async_copy(place_hbm, owned.at[1], local_sem.at[2 * CHUNKS + 3]),
     ]
-    table_rows, lanes = table.shape[0], TABLE_LANES
+    table_rows = table.shape[0]
+    table_start = pl.multiple_of(me_col * table_rows, 16)
     table_copies = [
         pltpu.make_async_copy(
-            tables_hbm.at[pl.ds(j * table_rows, table_rows), :],
-            table.at[:, pl.ds(j * lanes, lanes)],
-            table_sem.at[j],
-        )
-        for j in range(table.shape[1] // lanes)
+            tables_hbm.at[pl.ds(table_start, table_rows), :], table, table_sem.at[0]
+        )
     ]
-    mix_start = table_rows * len(table_copies) + me_row * mix.shape[0]
+    mix_start = table_rows * cols_n + me_row * mix.shape[0]
     mix_copy = pltpu.make_async_copy(
         tables_hbm.at[pl.ds(pl.multiple_of(mix_start, 16), mix.shape[0]), pl.ds(0, mix.shape[1])],
         mix,
@@ -317,11 +313,7 @@
 
     for copy in table_copies + [mix_copy]:
         copy.wait()
-    terms = table[2 * cols_dev :, :].astype(jnp.float32)
-    row = lax.broadcasted_iota(jnp.int32, terms.shape, 0)
-    twiddle_pair = jnp.sum(jnp.where(row // 2 == me_col, terms, 0.0), axis=0, keepdims=True)
-    mix_rows = mix.shape[0] // CHUNKS
-    cosine, sine = twiddle_pair[:, :cols_dev], twiddle_pair[:, cols_dev:]
+    mix_side = mix.shape[0]
 
     gathers = []
 
@@ -374,25 +366,22 @@
     sends = []
 
     def section_stage(h):
-        for copy in gathers[h][1:]:
-            copy.wait_recv()
-        sum_real = sum_imag = None
+        spectrum = None
         for d in range(cols_n):
-            turn = lax.rem(col_blocks[d] * me_col, cols_n)
-            cos_turn = jnp.where(turn == 0, 1.0, jnp.where(turn == 2, -1.0, 0.0))
-            sin_turn = jnp.where(turn == 1, 1.0, jnp.where(turn == 3, -1.0, 0.0))
-            value = dense[h, d].astype(jnp.float32)
-            real, imag = value * cos_turn, value * (-sin_turn)
-            sum_real = real if d == 0 else sum_real + real
-            sum_imag = imag if d == 0 else sum_imag + imag
-        section_one = jnp.concatenate(
-            [sum_real * cosine + sum_imag * sine, sum_imag * cosine - sum_real * sine], 1
-        ).astype(jnp.bfloat16)
-        spectrum = jnp.dot(section_one, table[0 : 2 * cols_dev, :], preferred_element_type=jnp.float32)
+            if d == 1:
+                gathers[h][1].wait_recv()
+            if d == 3:
+                gathers[h][2].wait_recv()
+            term = jnp.dot(
+                dense[h, d],
+                table[d * cols_dev : (d + 1) * cols_dev, :],
+                preferred_element_type=jnp.float32,
+            )
+            spectrum = term if d == 0 else spectrum + term
         spectrum = spectrum.astype(jnp.bfloat16)
         stacked = jnp.concatenate([spectrum[:, :cols_dev], spectrum[:, cols_dev:]], 0)
         section_two = jnp.dot(
-            mix[h * mix_rows : (h + 1) * mix_rows, :], stacked, preferred_element_type=jnp.float32
+            mix[:, h * mix_side : (h + 1) * mix_side], stacked, preferred_element_type=jnp.float32
         )
         outgoing[h] = section_two.astype(jnp.bfloat16).reshape(outgoing.shape[1:])
         group = [
@@ -445,16 +434,16 @@
 
 def final_kernel(final_ref, section_hbm, psf_ref, out_ref, section, sems):
     rows_dev = psf_ref.shape[0]
-    depth = section.shape[0] // CHUNKS
+    depth = section.shape[0] // 2
     copies = []
-    for h in range(CHUNKS):
+    for h in range(2):
         rows = pl.ds(h * depth, depth)
         copies.append(
             pltpu.make_async_copy(section_hbm.at[rows, :], section.at[rows, :], sems.at[h])
         )
         copies[h].start()
     result = None
-    for h in range(CHUNKS):
+    for h in range(2):
         copies[h].wait()
         at = slice(h * depth, h * depth + depth)
         term = jnp.dot(final_ref[:, at], section[at, :], preferred_element_type=jnp.float32)
@@ -483,7 +472,7 @@
         functools.partial(exchange_kernel, rows_n, cols_n, tile_side, bands, per_row),
         out_shape=jax.ShapeDtypeStruct((CHUNKS, rows_n, width, cols_dev), bf16),
         in_specs=[anywhere] * 4,
-        out_specs=vmem,
+        out_specs=anywhere,
         scratch_shapes=[
             pltpu.VMEM((2, 1, tile_count), jnp.int32),
             pltpu.VMEM(tile_density.shape, bf16),
@@ -493,8 +482,8 @@
             pltpu.VMEM((CHUNKS, rows_n, tile_count, chunk), bf16),
             pltpu.VMEM((CHUNKS, cols_n, step_rows * rows_n * bands, cols_dev), bf16),
             pltpu.VMEM((CHUNKS, rows_n, width, cols_dev), bf16),
-            pltpu.VMEM((2 * cols_dev + 16, 2 * cols_dev), bf16),
-            pltpu.VMEM((CHUNKS * mix_side, mix_side), bf16),
+            pltpu.VMEM((cols_n * cols_dev, 2 * cols_dev), bf16),
+            pltpu.VMEM((mix_side, CHUNKS * mix_side), bf16),
             dma((rows_n,)),
             dma((rows_n,)),
             dma((CHUNKS, rows_n)),
@@ -504,7 +493,7 @@
             dma((CHUNKS, rows_n)),
             dma((CHUNKS, rows_n)),
             dma((2 * CHUNKS + 4,)),
-            dma((2 * cols_dev // TABLE_LANES,)),
+            dma((1,)),
         ],
         compiler_params=pltpu.CompilerParams(
             collective_id=0, has_side_effects=True, vmem_limit_bytes=56 << 20
@@ -520,8 +509,8 @@
         out_shape=jax.ShapeDtypeStruct((rows_dev, 2, cols_dev), jnp.float32),
         in_specs=[vmem, anywhere, vmem],
         out_specs=vmem,
-        scratch_shapes=[pltpu.VMEM((2 * rows_dev, cols_dev), bf16), dma((CHUNKS,))],
-        compiler_params=pltpu.CompilerParams(vmem_limit_bytes=56 << 20),
+        scratch_shapes=[pltpu.VMEM((2 * rows_dev, cols_dev), bf16), dma((2,))],
+        compiler_params=pltpu.CompilerParams(vmem_limit_bytes=53 << 20),
     )(final, section.reshape(2 * rows_dev, cols_dev), psf_spectrum)
 
 

time: 40.9 us -> 38.5 us (0.941)
  Pallas kernels: 40.5 us -> 38.4 us
    pallas_call x1, Pallas kernels: 3.7 us -> 2.59 us  [on_device_kernels(): pl.pallas_call(final_kernel, out_shape=jax.ShapeDtypeStruct((rows_dev, 2,...]
    pallas_call x1, Pallas kernels: 36.8 us -> 35.8 us  [on_device_kernels(): pl.pallas_call(functools.partial(exchange_kernel, rows_n, cols_n, tile_si...]
where the time goes in v7:
time: 38.5 us; the launch traced here: 38.4 us
  Pallas kernels  38.4 us (100%)
    pallas_call x1, Pallas kernels, on_device_kernels(): pl.pallas_call(functools.partial(exchange_kernel, rows_n, cols_n, tile_si...  35.8 us
    pallas_call x1, Pallas kernels, on_device_kernels(): pl.pallas_call(final_kernel, out_shape=jax.ShapeDtypeStruct((rows_dev, 2,...  2.59 us

profile of v7, /device:TPU:0, one launch (start us, length us, event | category | flops | bytes accessed | tf_op | source)
XLA Modules:
  0.0 38.4 jit_solution(6140398415578347918)
XLA Ops:
  0.0 0.0 copy-start
  0.0 0.0 copy-start.1
  0.0 35.8 %shard_map.64 = bf16[4,8,16,512]{3,2,1,0:T(8,128)(2,1)} custom-call(bf16[64,64,64]{2,1,0:T(8,128)(2,1)} %tiles_hbm.1, s32[1,64]{1,0:T(1,128)} %bitcast.4, s32[1,64]{1,0:T(1,128)} %bitcast.5, bf16[9216,1024]{1,0:T(8,128)(2,1)} %constant.4.clone.tables_hbm), custom_call_target="tpu_custom_call" | custom-call | tf_op jit(solution)/shard_map/pallas_call | solution.py:471
  35.8 0.0 copy-done
  35.8 0.0 copy-done.1
  35.8 2.6 %shard_map.65 = f32[256,2,512]{2,1,0:T(2,128)} custom-call(bf16[512,512]{1,0:T(8,128)(2,1)S(1)} %copy-done, bf16[512,512]{1,0:T(8,128)(2,1)} %bitcast.3, bf16[256,512]{1,0:T(8,128)(2,1)S(1)} %copy-done.1), custom_call_target="tpu_custom_call" | custom-call | tf_op jit(solution)/shard_map/pallas_call | solution.py:507
Async XLA Ops:
  0.0 35.8 %copy-start = (bf16[512,512]{1,0:T(8,128)(2,1)S(1)}, bf16[512,512]{1,0:T(8,128)(2,1)}, u32[]{:S(2)}) copy-start(bf16[512,512]{1,0:T(8,128)(2,1)} %constant.5.clone.final_ref) | copy-start | bytes 1572868
  0.0 35.8 %copy-start.1 = (bf16[256,512]{1,0:T(8,128)(2,1)S(1)}, bf16[256,512]{1,0:T(8,128)(2,1)}, u32[]{:S(2)}) copy-start(bf16[256,512]{1,0:T(8,128)(2,1)} %psf_ref.1) | copy-start | bytes 786436

commit v8 on v7

--- a/solution.py
+++ b/solution.py
@@ -140,6 +140,7 @@
         and 2 * tile_side * (rows_dev // tile_side) <= 2 * cols_dev
         and 2 * tile_side // CHUNKS * (rows_dev // tile_side) % 128 == 0
         and cols_n * cols_dev <= 2048
+        and tile_side % (16 * CHUNKS) == 0
         and rows_n * rows_dev * cols_dev * 2 <= 1 << 22
     )
 
@@ -147,8 +148,7 @@
 def constants(rows_n, cols_n, tile_side, rows_dev, cols_dev):
     slab_cols, grid_rows = cols_dev * cols_n, rows_dev * rows_n
     bands = rows_dev // tile_side
-    band_rows = tile_side // rows_n
-    step_rows = band_rows // CHUNKS
+    step_rows = tile_side // rows_n // CHUNKS
 
     def parts(phase, factor):
         angles = 2.0 * np.pi * phase
@@ -165,8 +165,8 @@
     row_tables = np.concatenate([re, im], 2)
     b = (
         tile_side * np.arange(bands)[None, None, None, :]
-        + band_rows * np.arange(rows_n)[:, None, None, None]
-        + step_rows * np.arange(CHUNKS)[None, :, None, None]
+        + step_rows * np.arange(rows_n)[:, None, None, None]
+        + step_rows * rows_n * np.arange(CHUNKS)[None, :, None, None]
         + np.arange(step_rows)[None, None, :, None]
     )
     u = np.arange(rows_n)
@@ -201,7 +201,7 @@
     tiles_hbm, dest_hbm, place_hbm, tables_hbm,
     out_ref,
     owned, raw, wide, banded, labels, arrived, dense, outgoing, table, mix,
-    label_send, label_recv, a_send, a_recv, g_send, g_recv, e_send, e_recv, local_sem, table_sem,
+    label_send, label_recv, a_send, a_recv, g_send, g_recv, e_send, e_recv, local_sem, table_sem, raw_sem,
 ):
     me_row, me_col = lax.axis_index("rows"), lax.axis_index("cols")
     tiles = tiles_hbm.shape[0]
@@ -209,6 +209,7 @@
     cols_dev = per_row * tile_side
     row_peers = [lax.rem(me_row + d, rows_n) for d in range(rows_n)]
     row_sources = [lax.rem(me_row + rows_n - d, rows_n) for d in range(rows_n)]
+    far_first = sorted(range(1, rows_n), key=lambda d: abs(2 * d - rows_n))
     sibling = me_col + 1 - 2 * lax.rem(me_col, 2)
     col_blocks = [me_col, sibling, lax.rem(me_col + 2, cols_n), lax.rem(sibling + 2, cols_n)]
 
@@ -218,8 +219,14 @@
     for d in range(1, 3):
         pl.semaphore_signal(barrier, inc=1, device_id=(me_row, col_blocks[d]), device_id_type=MESH)
 
-    raw_copy = pltpu.make_async_copy(tiles_hbm, raw, local_sem.at[CHUNKS + 1])
-    raw_copy.start()
+    group_rows = tile_side // CHUNKS
+    raw_copies = []
+    for h in range(CHUNKS):
+        rows = pl.ds(h * group_rows, group_rows)
+        raw_copies.append(
+            pltpu.make_async_copy(tiles_hbm.at[:, rows, :], raw.at[h], raw_sem.at[h])
+        )
+        raw_copies[h].start()
     owned_copies = [
         pltpu.make_async_copy(dest_hbm, owned.at[0], local_sem.at[2 * CHUNKS + 2]),
         pltpu.make_async_copy(place_hbm, owned.at[1], local_sem.at[2 * CHUNKS + 3]),
@@ -250,19 +257,21 @@
         labels.shape[1:],
     )
     low_lanes = lax.broadcasted_iota(jnp.int32, (max(tiles, rows_n * bands), 128), 1) < tile_side
-    raw_copy.wait()
-    wide[:, 0:tile_side] = raw[...].reshape(tiles * tile_side, tile_side).astype(jnp.float32)
     own_copies = [
         pltpu.make_async_copy(banded.at[h, me_row], arrived.at[h, 0], local_sem.at[h])
         for h in range(CHUNKS)
     ]
 
     def band_stage(h):
+        raw_copies[h].wait()
+        wide[h, :, 0:tile_side] = (
+            raw[h].reshape(tiles * group_rows, tile_side).astype(jnp.float32)
+        )
         for owner in range(rows_n):
             for pair in range(chunk // 128):
-                row = (owner * CHUNKS + h) * (chunk // tile_side) + 2 * pair
-                first = wide[pl.ds(row, tiles, stride=tile_side), :]
-                second = wide[pl.ds(row + 1, tiles, stride=tile_side), :]
+                row = owner * (chunk // tile_side) + 2 * pair
+                first = wide[h, pl.ds(row, tiles, stride=group_rows), :]
+                second = wide[h, pl.ds(row + 1, tiles, stride=group_rows), :]
                 both = jnp.where(low_lanes[:tiles], first, pltpu.roll(second, tile_side, 1))
                 banded[h, owner, :, 128 * pair : 128 * pair + 128] = both.astype(jnp.bfloat16)
         own_copies[h].start()
@@ -291,7 +300,7 @@
         )
         for d in range(1, rows_n)
     ]
-    band_copies = [[band_copy(h, d) for d in range(1, rows_n)] for h in range(CHUNKS)]
+    band_copies = [[band_copy(h, d) for d in far_first] for h in range(CHUNKS)]
     for copy in label_copies:
         copy.start()
     def band_start(h):
@@ -393,7 +402,7 @@
                 device_id=(row_peers[d], me_col),
                 device_id_type=MESH,
             )
-            for d in range(1, rows_n)
+            for d in far_first
         ]
         for copy in group:
             copy.start()
@@ -475,8 +484,8 @@
         out_specs=anywhere,
         scratch_shapes=[
             pltpu.VMEM((2, 1, tile_count), jnp.int32),
-            pltpu.VMEM(tile_density.shape, bf16),
-            pltpu.VMEM((tile_count * tile_side, 128), jnp.float32),
+            pltpu.VMEM((CHUNKS, tile_count, tile_side // CHUNKS, tile_side), bf16),
+            pltpu.VMEM((CHUNKS, tile_count * tile_side // CHUNKS, 128), jnp.float32),
             pltpu.VMEM((CHUNKS, rows_n, tile_count, chunk), bf16),
             pltpu.VMEM((rows_n, 8, 128), jnp.int32),
             pltpu.VMEM((CHUNKS, rows_n, tile_count, chunk), bf16),
@@ -494,6 +503,7 @@
             dma((CHUNKS, rows_n)),
             dma((2 * CHUNKS + 4,)),
             dma((1,)),
+            dma((CHUNKS,)),
         ],
         compiler_params=pltpu.CompilerParams(
             collective_id=0, has_side_effects=True, vmem_limit_bytes=56 << 20

time: 38.5 us -> 37.5 us (0.974)
  Pallas kernels: 38.4 us -> 37.3 us
    pallas_call x1, Pallas kernels: 35.8 us -> 34.7 us  [on_device_kernels(): pl.pallas_call(functools.partial(exchange_kernel, rows_n, cols_n, tile_si...]
where the time goes in v8:
time: 37.5 us; the launch traced here: 37.4 us
  Pallas kernels  37.3 us (99%)
    pallas_call x1, Pallas kernels, on_device_kernels(): pl.pallas_call(functools.partial(exchange_kernel, rows_n, cols_n, tile_si...  34.7 us
    pallas_call x1, Pallas kernels, on_device_kernels(): pl.pallas_call(final_kernel, out_shape=jax.ShapeDtypeStruct((rows_dev, 2,...  2.59 us

profile of v8, /device:TPU:0, one launch (start us, length us, event | category | flops | bytes accessed | tf_op | source)
XLA Modules:
  0.0 37.4 jit_solution(5215029275866853569)
XLA Ops:
  0.0 0.0 copy-start
  0.0 0.0 copy-start.1
  0.0 34.7 %shard_map.64 = bf16[4,8,16,512]{3,2,1,0:T(8,128)(2,1)} custom-call(bf16[64,64,64]{2,1,0:T(8,128)(2,1)} %tiles_hbm.1, s32[1,64]{1,0:T(1,128)} %bitcast.4, s32[1,64]{1,0:T(1,128)} %bitcast.5, bf16[9216,1024]{1,0:T(8,128)(2,1)} %constant.4.clone.tables_hbm), custom_call_target="tpu_custom_call" | custom-call | tf_op jit(solution)/shard_map/pallas_call | solution.py:480
  34.7 0.0 copy-done
  34.8 0.0 copy-done.1
  34.8 2.6 %shard_map.65 = f32[256,2,512]{2,1,0:T(2,128)} custom-call(bf16[512,512]{1,0:T(8,128)(2,1)S(1)} %copy-done, bf16[512,512]{1,0:T(8,128)(2,1)} %bitcast.3, bf16[256,512]{1,0:T(8,128)(2,1)S(1)} %copy-done.1), custom_call_target="tpu_custom_call" | custom-call | tf_op jit(solution)/shard_map/pallas_call | solution.py:517
Async XLA Ops:
  0.0 34.7 %copy-start = (bf16[512,512]{1,0:T(8,128)(2,1)S(1)}, bf16[512,512]{1,0:T(8,128)(2,1)}, u32[]{:S(2)}) copy-start(bf16[512,512]{1,0:T(8,128)(2,1)} %constant.5.clone.final_ref) | copy-start | bytes 1572868
  0.0 34.8 %copy-start.1 = (bf16[256,512]{1,0:T(8,128)(2,1)S(1)}, bf16[256,512]{1,0:T(8,128)(2,1)}, u32[]{:S(2)}) copy-start(bf16[256,512]{1,0:T(8,128)(2,1)} %psf_ref.1) | copy-start | bytes 786436

commit v9 on v8

--- a/solution.py
+++ b/solution.py
@@ -413,14 +413,13 @@
         sends.append((group, own))
 
     for h in range(CHUNKS):
+        if h > 0:
+            forward_stage(h - 1)
         density_stage(h)
         if h > 0:
-            forward_stage(h - 1)
-        if h > 1:
-            section_stage(h - 2)
+            section_stage(h - 1)
     forward_stage(CHUNKS - 1)
-    for h in range(CHUNKS - 2, CHUNKS):
-        section_stage(h)
+    section_stage(CHUNKS - 1)
 
     for copy in label_copies:
         copy.wait_send()

time: 37.5 us -> 39.5 us (1.053)
  Pallas kernels: 37.3 us -> 39.3 us
    pallas_call x1, Pallas kernels: 34.7 us -> 36.7 us  [on_device_kernels(): pl.pallas_call(functools.partial(exchange_kernel, rows_n, cols_n, tile_si...]
where the time goes in v9:
time: 39.5 us; the launch traced here: 39.3 us
  Pallas kernels  39.3 us (99%)
    pallas_call x1, Pallas kernels, on_device_kernels(): pl.pallas_call(functools.partial(exchange_kernel, rows_n, cols_n, tile_si...  36.7 us
    pallas_call x1, Pallas kernels, on_device_kernels(): pl.pallas_call(final_kernel, out_shape=jax.ShapeDtypeStruct((rows_dev, 2,...  2.59 us

profile of v9, /device:TPU:0, one launch (start us, length us, event | category | flops | bytes accessed | tf_op | source)
XLA Modules:
  0.0 39.3 jit_solution(14296582813025581131)
XLA Ops:
  0.0 0.0 copy-start
  0.0 0.0 copy-start.1
  0.0 36.7 %shard_map.64 = bf16[4,8,16,512]{3,2,1,0:T(8,128)(2,1)} custom-call(bf16[64,64,64]{2,1,0:T(8,128)(2,1)} %tiles_hbm.1, s32[1,64]{1,0:T(1,128)} %bitcast.4, s32[1,64]{1,0:T(1,128)} %bitcast.5, bf16[9216,1024]{1,0:T(8,128)(2,1)} %constant.4.clone.tables_hbm), custom_call_target="tpu_custom_call" | custom-call | tf_op jit(solution)/shard_map/pallas_call | solution.py:479
  36.7 0.0 copy-done
  36.7 0.0 copy-done.1
  36.7 2.6 %shard_map.65 = f32[256,2,512]{2,1,0:T(2,128)} custom-call(bf16[512,512]{1,0:T(8,128)(2,1)S(1)} %copy-done, bf16[512,512]{1,0:T(8,128)(2,1)} %bitcast.3, bf16[256,512]{1,0:T(8,128)(2,1)S(1)} %copy-done.1), custom_call_target="tpu_custom_call" | custom-call | tf_op jit(solution)/shard_map/pallas_call | solution.py:516
Async XLA Ops:
  0.0 36.7 %copy-start = (bf16[512,512]{1,0:T(8,128)(2,1)S(1)}, bf16[512,512]{1,0:T(8,128)(2,1)}, u32[]{:S(2)}) copy-start(bf16[512,512]{1,0:T(8,128)(2,1)} %constant.5.clone.final_ref) | copy-start | bytes 1572868
  0.0 36.7 %copy-start.1 = (bf16[256,512]{1,0:T(8,128)(2,1)S(1)}, bf16[256,512]{1,0:T(8,128)(2,1)}, u32[]{:S(2)}) copy-start(bf16[256,512]{1,0:T(8,128)(2,1)} %psf_ref.1) | copy-start | bytes 786436
